TPU v7x, 128 devices: a whole 4x4x4 slice. The times are simulated.
128 devices in a mesh: grp: 16 (over z, x), tp: 8 (over y, core).
Axes of the slice: x: 4, y: 4, z: 4, core: 2. Of those that a mesh axis runs over, the one named last changes fastest.
Arguments:
- queries: bfloat16 [128, 48, 128], P('grp', 'tp'), may hold values from -32 to 32
- kv_cache: bfloat16 [128, 2, 8, 384, 128], P('grp', None, 'tp'), may hold values from -6 to 6
- new_kv: bfloat16 [128, 2, 8, 128], P('grp', None, 'tp'), may hold values from -6 to 6
- lengths: int32 [128], P('grp'), may hold values from 1 to 383, as said below
- residual: bfloat16 [128, 6144], P('grp', 'tp'), may hold values from -9 to 9
- w_out: bfloat16 [6144, 6144], P('tp'), may hold values from -0.078125 to 0.078125
- norm_gain: bfloat16 [6144], P('tp'), may hold values from 0.099609375 to 1.8984375
- expert_ids: int32 [128, 2], P('grp'), may hold values from 0 to 3, all different within a row; in each aligned block of 8 rows (0 to 7, 8 to 15, ...) at most 8 rows name the same one
- gate_w: float32 [128, 2], P('grp'), may hold values from 0.25 to 1
- w_inner: bfloat16 [6144, 2, 32768], P(None, None, ('grp', 'tp')), may hold values from -0.078125 to 0.078125
- w_down: bfloat16 [32768, 6144], P(('grp', 'tp')), may hold values from -0.0625 to 0.0625
- mig_rows: int32 [8], replicated, may hold values from 0 to 127, as said below
- mig_dest: int32 [8], replicated, may hold values from 0 to 15, as said below
Outputs:
- mixed: bfloat16 [128, 6144], P('grp', 'tp')
- landed: bfloat16 [16, 2, 8, 384, 128], P('grp', None, 'tp')
Inputs may be any that keep to these rules, and one draw needn't show every extreme that they name: `lengths`: the longest cache holds 383 tokens, so the new token always has a free position. `expert_ids`: each row names two different experts. `mig_rows`: the listed rows lie in distinct replicas. `mig_dest`: the destinations are distinct, and none is the replica that holds the row at the same position of the list.
All inputs are finite; a program needn't handle non-finite values.
Results may differ from a plain program's by a relative error of at most 0.012.
Values may be sent and summed in bfloat16 or wider, within the bound.
A program may use at most 128 MiB of HBM per device.

v0:
```python
import jax
import jax.numpy as jnp
from jax import lax
from jax.sharding import PartitionSpec as P

D = 6144
EXPERTS = 4
MIG = 8


def attend(queries, kv_block, fresh_kv, lengths):
    row_count, head_count, feature_dim = queries.shape
    kv_heads = kv_block.shape[2]
    span_len = kv_block.shape[3]
    grouped = queries.reshape(row_count, kv_heads, head_count // kv_heads, feature_dim)
    scaling = feature_dim ** (-0.5)
    scores = (
        jnp.einsum("rkgd,rkpd->rkgp", grouped, kv_block[:, 0], preferred_element_type=jnp.float32)
        * scaling
    )
    own_score = (
        jnp.einsum("rkgd,rkd->rkg", grouped, fresh_kv[:, 0], preferred_element_type=jnp.float32)
        * scaling
    )
    visible = (jnp.arange(span_len, dtype=jnp.int32)[None, :] < lengths[:, None])[:, None, None, :]
    masked = jnp.where(visible, scores, -jnp.inf)
    highest = jnp.maximum(jnp.max(masked, axis=-1), own_score)
    spread = jnp.where(visible, jnp.exp(masked - highest[..., None]), 0.0)
    own_exp = jnp.exp(own_score - highest)
    denominator = jnp.sum(spread, axis=-1) + own_exp
    weights = (spread / denominator[..., None]).astype(jnp.bfloat16)
    own_weight = (own_exp / denominator).astype(jnp.bfloat16)
    mixture = jnp.einsum(
        "rkgp,rkpd->rkgd", weights, kv_block[:, 1], preferred_element_type=jnp.float32
    )
    mixture = (
        mixture
        + own_weight.astype(jnp.float32)[..., None]
        * fresh_kv[:, 1].astype(jnp.float32)[:, :, None, :]
    )
    return mixture.astype(jnp.bfloat16).reshape(row_count, head_count * feature_dim)


def seal(kv_slab, fresh_kv, length):
    positions = jnp.arange(kv_slab.shape[-2], dtype=jnp.int32)[:, None]
    return jnp.where(
        positions < length,
        kv_slab,
        jnp.where(positions == length, fresh_kv[:, :, None, :], jnp.zeros_like(kv_slab)),
    )


def body(
    queries,
    kv_cache,
    new_kv,
    lengths,
    residual,
    w_out,
    norm_gain,
    expert_ids,
    gate_w,
    w_inner,
    w_down,
    mig_rows,
    mig_dest,
):
    row_count = queries.shape[0]
    replicas = lax.axis_size("grp")
    tensor = lax.axis_size("tp")
    members = replicas // EXPERTS
    local_width = residual.shape[1]
    hidden_dev = w_down.shape[0]
    group_index = lax.axis_index("grp")
    source_rep = mig_rows // row_count
    leaving = source_rep == group_index
    migrant = jnp.sum(jnp.where(leaving, jnp.arange(MIG, dtype=jnp.int32), 0))
    has_leaver = jnp.any(leaving)
    local_row = jnp.clip(mig_rows[migrant] - group_index * row_count, 0, row_count - 1)
    kv_slab = seal(
        lax.dynamic_index_in_dim(kv_cache, local_row, 0, keepdims=False),
        lax.dynamic_index_in_dim(new_kv, local_row, 0, keepdims=False),
        lengths[local_row],
    )
    kv_slab = jnp.where(has_leaver, kv_slab, jnp.zeros_like(kv_slab))
    target = jnp.logical_and(jnp.arange(replicas, dtype=jnp.int32) == mig_dest[migrant], has_leaver)
    outgoing_slabs = jnp.where(
        target[:, None, None, None, None], kv_slab[None], jnp.zeros_like(kv_slab)[None]
    )
    received = lax.all_to_all(outgoing_slabs, "grp", split_axis=0, concat_axis=0, tiled=True)
    arriving = mig_dest == group_index
    sender = jnp.sum(jnp.where(arriving, source_rep, 0))
    landed = jnp.where(
        jnp.any(arriving),
        lax.dynamic_index_in_dim(received, sender, 0, keepdims=False),
        jnp.zeros_like(kv_slab),
    )
    heads_out = attend(queries, kv_cache, new_kv, lengths)
    partial_value = jnp.dot(heads_out, w_out, preferred_element_type=jnp.float32)
    attended = lax.psum_scatter(partial_value, "tp", scatter_dimension=1, tiled=True)
    hidden_state = residual.astype(jnp.float32) + attended
    squares = lax.psum(jnp.sum(hidden_state * hidden_state, axis=1), "tp")
    normed = (
        hidden_state
        * lax.rsqrt(squares / D + 1e-05)[:, None]
        * norm_gain.astype(jnp.float32)[None, :]
    ).astype(jnp.bfloat16)
    assigned = (
        expert_ids[:, :, None] == jnp.arange(EXPERTS, dtype=jnp.int32)[None, None, :]
    ).astype(jnp.int32)
    flat_hits = assigned.reshape(row_count * 2, EXPERTS)
    before = jnp.cumsum(flat_hits, axis=0) - flat_hits
    slot_index = jnp.sum(before * flat_hits, axis=1).reshape(row_count, 2)
    slot_hot = (
        slot_index[:, :, None] == jnp.arange(row_count, dtype=jnp.int32)[None, None, :]
    ).astype(jnp.float32)
    placing = jnp.einsum("rke,rkc->ecr", assigned.astype(jnp.float32), slot_hot)
    weighing = jnp.einsum(
        "rke,rkc->rec",
        assigned.astype(jnp.float32) * gate_w[:, :, None],
        slot_hot,
        precision=lax.Precision.HIGHEST,
    )
    weighing = jnp.broadcast_to(
        weighing[:, :, None, :], (row_count, EXPERTS, members, row_count)
    ).reshape(row_count, replicas, row_count)
    inner_mat = w_inner.reshape(w_inner.shape[0], 2 * hidden_dev)
    whole_rows = lax.all_gather(normed, "tp", axis=1, tiled=True)
    share_rows = row_count // tensor
    own_slots = lax.dynamic_slice_in_dim(placing, lax.axis_index("tp") * share_rows, share_rows, 1)
    portion = jnp.einsum(
        "ecr,rd->ecd",
        own_slots.astype(jnp.bfloat16),
        whole_rows,
        preferred_element_type=jnp.float32,
    ).astype(jnp.bfloat16)
    full_width = portion.shape[2]
    outgoing = jnp.broadcast_to(
        portion[:, None, None], (EXPERTS, members, tensor, share_rows, full_width)
    ).reshape(replicas * tensor, share_rows, full_width)
    arrived = lax.all_to_all(outgoing, ("grp", "tp"), split_axis=0, concat_axis=0, tiled=True)
    projected = jnp.dot(
        arrived.reshape(replicas * row_count, full_width),
        inner_mat,
        preferred_element_type=jnp.float32,
    )
    gate_part = projected[:, :hidden_dev]
    up_part = projected[:, hidden_dev:]
    activated = (jax.nn.silu(gate_part) * up_part).astype(jnp.bfloat16)
    down_split = w_down.reshape(hidden_dev, tensor, local_width)
    down_term = jnp.einsum(
        "gcf,ftd->gtcd",
        activated.reshape(replicas, row_count, hidden_dev),
        down_split,
        preferred_element_type=jnp.float32,
    ).reshape(replicas * tensor, row_count, local_width)
    returned = lax.all_to_all(down_term, ("grp", "tp"), split_axis=0, concat_axis=0, tiled=True)
    expert_out = jnp.sum(returned.reshape(replicas, tensor, row_count, local_width), axis=1)
    moe_out = jnp.einsum("rjc,jcd->rd", weighing, expert_out, precision=lax.Precision.HIGHEST)
    result = (hidden_state + moe_out).astype(jnp.bfloat16)
    return (result, landed[None])


def solution(mesh):
    in_specs = (
        P("grp", "tp", None),
        P("grp", None, "tp", None, None),
        P("grp", None, "tp", None),
        P("grp"),
        P("grp", "tp"),
        P("tp", None),
        P("tp"),
        P("grp", None),
        P("grp", None),
        P(None, None, ("grp", "tp")),
        P(("grp", "tp"), None),
        P(),
        P(),
    )
    out_specs = (P("grp", "tp"), P("grp", None, "tp", None, None))
    return jax.shard_map(body, mesh=mesh, in_specs=in_specs, out_specs=out_specs, check_vma=False)
```

profile of v0, /device:TPU:0, one launch (start us, length us, event | category | flops | bytes accessed | tf_op | source)
XLA Modules:
  0.0 225.2 jit_solution(12104857314477042617)
XLA Ops:
  7.2 0.7 iota_compare_fusion
  7.9 0.8 slice_convert_fusion
  8.7 0.8 fusion.22
  9.5 1.6 fusion.49
  11.2 0.2 fusion.15
  11.4 1.4 fusion.9
  12.8 5.7 %fusion.25 = f32[8,6144]{1,0:T(8,128)} fusion(bf16[768,6144]{1,0:T(8,128)(2,1)} %param.18, bf16[1,8,6,128]{3,2,1,0:T(8,128)(2,1)S(1)} %fusion.9), kind=kOutput, calls=%fused_computation.40 | convolution fusion | flops 75497472 | bytes 9646080 | tf_op jit(solution)/shard_map/dot_general | solution.py:99
  18.6 0.1 copy.49
  18.7 0.1 eq.67
  18.9 0.2 select_reduce_fusion
  19.2 0.3 fusion.29
  19.5 32.2 %reduce-scatter.2.cloned.1.call-done = f32[8,768]{1,0:T(8,128)} async-done(((f32[8,6144]{1,0:T(8,128)}), f32[8,768]{1,0:T(8,128)}) %reduce-scatter.2.cloned.1.call-update) | async-done | bytes 24592 | tf_op jit(solution)/shard_map/reduce_scatter | solution.py:100
  51.6 0.9 multiply_reduce_fusion
  52.5 0.1 copy.53
  52.6 12.7 %psum.7 = f32[8]{0:T(128)S(1)} all-reduce(f32[8]{0:T(128)S(1)} %multiply_reduce_fusion), channel_id=1, replica_groups=mesh['grp'=16,'tp'=8] {'tp'}, use_global_device_ids=true, to_apply=%region_6.7 | all-reduce | flops 8 | bytes 64 | tf_op jit(solution)/shard_map/psum | solution.py:102
  65.3 0.8 multiply_convert_fusion
  66.1 12.7 %all_gather.3 = bf16[8,6144]{1,0:T(8,128)(2,1)S(1)} all-gather(bf16[8,768]{1,0:T(8,128)(2,1)S(1)} %multiply_convert_fusion), channel_id=1, replica_groups=mesh['grp'=16,'tp'=8] {'tp'}, dimensions={1}, use_global_device_ids=true | all-gather | bytes 110592 | tf_op jit(solution)/shard_map/all_gather | solution.py:128
  78.8 0.1 convolution_convert_fusion
  79.0 0.1 broadcast_in_dim.109
  79.1 0.5 broadcast.172
  79.6 1.9 reduce.4
  81.5 2.1 reshape.188
  83.6 8.5 %all-to-all-start = ((bf16[128,2,3072]{2,1,0:T(2,128)(2,1)}), bf16[128,2,3072]{2,1,0:T(2,128)(2,1)S(1)}, u32[]{:S(2)}, u32[]{:S(2)}) async-start(bf16[128,2,3072]{2,1,0:T(2,128)(2,1)} %reshape.188), calls=%async_computation.1 | async-start | bytes 3145728 | tf_op jit(solution)/shard_map/all_to_all | solution.py:141
  92.1 0.6 fusion.45
  94.7 0.6 dynamic_slice.26
  95.3 0.6 dynamic_slice.25
  96.6 0.7 dynamic_slice.27
  97.2 0.7 fusion.44
  97.9 0.6 compare_reduce_fusion
  98.5 1.3 compare_and_fusion
  99.8 0.6 iota_compare_fusion.5
  100.4 1.7 select_bitcast_fusion
  102.2 2.0 broadcast_select_fusion
  104.2 12.7 %all-to-all-done = bf16[128,2,3072]{2,1,0:T(2,128)(2,1)S(1)} async-done(((bf16[128,2,3072]{2,1,0:T(2,128)(2,1)}), bf16[128,2,3072]{2,1,0:T(2,128)(2,1)S(1)}, u32[]{:S(2)}, u32[]{:S(2)}) %all-to-all-start) | async-done | bytes 1572896 | tf_op jit(solution)/shard_map/all_to_all | solution.py:141
  116.9 1.2 copy-done
  118.0 4.5 %all-to-all-start.2 = ((bf16[16,2,1,384,128]{4,3,2,1,0:T(8,128)(2,1)}), bf16[16,2,1,384,128]{4,3,2,1,0:T(8,128)(2,1)}, u32[]{:S(2)}, u32[]{:S(2)}) async-start(bf16[16,2,1,384,128]{4,3,2,1,0:T(8,128)(2,1)} %broadcast_select_fusion), calls=%async_computation.3 | async-start | bytes 6291456 | tf_op jit(solution)/shard_map/all_to_all | solution.py:90
  122.6 6.5 %copy.65 = bf16[768,8,2,256]{3,1,2,0:T(8,128)(2,1)} copy(bf16[768,8,2,256]{3,2,1,0:T(2,128)(2,1)} %bitcast.75) | data formatting | bytes 12582912
  129.1 9.1 %reshape.189 = bf16[128,1,6144]{2,1,0:T(2,128)(2,1)S(1)} reshape(bf16[128,2,3072]{2,1,0:T(2,128)(2,1)} %copy-done) | data formatting | bytes 3145728
  138.2 4.2 %fusion.2 = f32[128,512]{1,0:T(8,128)S(1)} fusion(bf16[6144,512]{1,0:T(8,128)(2,1)} %bitcast.74, bf16[128,1,6144]{2,1,0:T(2,128)(2,1)S(1)} %reshape.189), kind=kOutput, calls=%fused_computation.6 | convolution fusion | flops 805306368 | bytes 8126464 | tf_op jit(solution)/shard_map/dot_general | solution.py:142
  142.4 2.3 %fusion = f32[16,8,8,768]{3,1,2,0:T(8,128)} fusion(bf16[32,8,8,768]{3,2,1,0:T(8,128)(2,1)S(1)} %bitcast.77, f32[128,512]{1,0:T(8,128)S(1)} %fusion.2), kind=kOutput, calls=%fused_computation.2 | convolution fusion | flops 402849792 | bytes 6553600 | tf_op jit(solution)/shard_map/gcf,ftd->gtcd/dot_general | solution.py:151
  144.6 24.6 %all-to-all-done.2 = bf16[16,2,1,384,128]{4,3,2,1,0:T(8,128)(2,1)} async-done(((bf16[16,2,1,384,128]{4,3,2,1,0:T(8,128)(2,1)}), bf16[16,2,1,384,128]{4,3,2,1,0:T(8,128)(2,1)}, u32[]{:S(2)}, u32[]{:S(2)}) %all-to-all-start.2) | async-done | bytes 3145760 | tf_op jit(solution)/shard_map/all_to_all | solution.py:90
  169.2 5.8 %all-to-all-start.1 = ((f32[128,8,768]{2,1,0:T(8,128)}), f32[128,8,768]{2,1,0:T(8,128)S(1)}, u32[]{:S(2)}, u32[]{:S(2)}) async-start(f32[128,8,768]{2,1,0:T(8,128)} %bitcast.16), calls=%async_computation.2 | async-start | bytes 6291456 | tf_op jit(solution)/shard_map/all_to_all | solution.py:157
  175.1 0.3 fusion.30
  177.4 0.6 compare_reduce_fusion.1
  178.0 2.3 %dynamic-slice_select_fusion = bf16[1,2,1,384,128]{4,3,2,1,0:T(8,128)(2,1)} fusion(bf16[16,2,1,384,128]{4,3,2,1,0:T(8,128)(2,1)} %all-to-all-done.2, s32[]{:T(128)S(6)} %select_n.102, pred[]{:T(512)} %compare_reduce_fusion.1), kind=kLoop, calls=%fused_computation.21 | loop fusion | flops 98304 | bytes 393221 | tf_op jit(solution)/shard_map/jit(_where)/select_n | solution.py:93
  180.3 36.4 %all-to-all-done.1 = f32[128,8,768]{2,1,0:T(8,128)S(1)} async-done(((f32[128,8,768]{2,1,0:T(8,128)}), f32[128,8,768]{2,1,0:T(8,128)S(1)}, u32[]{:S(2)}, u32[]{:S(2)}) %all-to-all-start.1) | async-done | bytes 3145760 | tf_op jit(solution)/shard_map/all_to_all | solution.py:157
  216.7 0.2 bitcast_reduce_fusion
  216.9 1.5 fusion.8
  (33 shorter events, 0.4 us)
Async XLA Ops:
  7.2 44.5 %reduce-scatter.2.cloned.1.call-start = ((), (), s32[]{:S(2)}) async-start(), calls=%async_computation.4 | async-start | bytes 221184 | tf_op jit(solution)/shard_map/reduce_scatter | solution.py:100
  12.8 5.8 %copy-start.5 = (s32[8,2]{0,1:T(2,128)S(1)}, s32[8,2]{0,1:T(2,128)}, u32[]{:S(2)}) copy-start(s32[8,2]{0,1:T(2,128)} %param.20) | copy-start | bytes 196
  12.8 6.2 %copy-start.4 = (bf16[768]{0:T(1024)(128)(2,1)S(1)}, bf16[768]{0:T(1024)(128)(2,1)}, u32[]{:S(2)}) copy-start(bf16[768]{0:T(1024)(128)(2,1)} %param.19) | copy-start | bytes 4612
  12.8 38.8 %copy-start.3 = (bf16[8,768]{1,0:T(8,128)(2,1)S(1)}, bf16[8,768]{1,0:T(8,128)(2,1)}, u32[]{:S(2)}) copy-start(bf16[8,768]{1,0:T(8,128)(2,1)} %param.17) | copy-start | bytes 36868
  81.5 10.6 %copy-start.8 = (s32[8]{0:T(128)S(1)}, s32[8]{0:T(128)}, u32[]{:S(2)}) copy-start(s32[8]{0:T(128)} %param.24) | copy-start | bytes 100
  81.5 10.6 %copy-start.9 = (s32[8]{0:T(128)S(1)}, s32[8]{0:T(128)}, u32[]{:S(2)}) copy-start(s32[8]{0:T(128)} %param.25) | copy-start | bytes 100
  81.5 15.1 %copy-start.7 = (s32[8]{0:T(128)S(1)}, s32[8]{0:T(128)}, u32[]{:S(2)}) copy-start(s32[8]{0:T(128)} %param.16) | copy-start | bytes 100
  83.6 33.2 %all-to-all-start = ((bf16[128,2,3072]{2,1,0:T(2,128)(2,1)}), bf16[128,2,3072]{2,1,0:T(2,128)(2,1)S(1)}, u32[]{:S(2)}, u32[]{:S(2)}) async-start(bf16[128,2,3072]{2,1,0:T(2,128)(2,1)} %reshape.188), calls=%async_computation.1 | async-start | bytes 3145728 | tf_op jit(solution)/shard_map/all_to_all | solution.py:141
  116.9 1.2 copy-start
  118.0 51.2 %all-to-all-start.2 = ((bf16[16,2,1,384,128]{4,3,2,1,0:T(8,128)(2,1)}), bf16[16,2,1,384,128]{4,3,2,1,0:T(8,128)(2,1)}, u32[]{:S(2)}, u32[]{:S(2)}) async-start(bf16[16,2,1,384,128]{4,3,2,1,0:T(8,128)(2,1)} %broadcast_select_fusion), calls=%async_computation.3 | async-start | bytes 6291456 | tf_op jit(solution)/shard_map/all_to_all | solution.py:90
  138.2 4.2 %copy-start.1 = (bf16[256,6144]{1,0:T(8,128)(2,1)S(1)}, bf16[256,6144]{1,0:T(8,128)(2,1)}, u32[]{:S(2)}) copy-start(bf16[256,6144]{1,0:T(8,128)(2,1)} %param.23) | copy-start | bytes 9437188
  169.2 5.8 %copy-start.6 = (f32[8,2]{0,1:T(2,128)S(1)}, f32[8,2]{0,1:T(2,128)}, u32[]{:S(2)}) copy-start(f32[8,2]{0,1:T(2,128)} %param.21) | copy-start | bytes 196
  169.2 47.5 %all-to-all-start.1 = ((f32[128,8,768]{2,1,0:T(8,128)}), f32[128,8,768]{2,1,0:T(8,128)S(1)}, u32[]{:S(2)}, u32[]{:S(2)}) async-start(f32[128,8,768]{2,1,0:T(8,128)} %bitcast.16), calls=%async_computation.2 | async-start | bytes 6291456 | tf_op jit(solution)/shard_map/all_to_all | solution.py:157
  175.0 41.9 %copy-start.2 = (f32[8,768]{1,0:T(8,128)S(1)}, f32[8,768]{1,0:T(8,128)}, u32[]{:S(2)}) copy-start(f32[8,768]{1,0:T(8,128)} %reduce-scatter.2.cloned.1.call-done) | copy-start | bytes 73732
Sparse Core Ops, SparseCore 0:
  18.7 32.8 reduce-scatter.1
where the time goes:
time: 227 us; the launch traced here: 225 us
  waiting for transfers between devices  106 us (47%)
  blocking collectives  25.4 us (11%)
  local copies, waits for them, and re-layouts  22.5 us (10%)
  between operations  18.9 us (8%)
  starting transfers between devices  18.8 us (8%)
  matrix products  18.3 us (8%)
  other arithmetic  15.5 us (7%)
    all_to_all x1, waiting for transfers between devices, body(): lax.all_to_all(down_term, ('grp', 'tp'), split_axis=0, concat_axis=0, til...  36.4 us
    reduce_scatter x1, waiting for transfers between devices, body(): lax.psum_scatter(partial_value, 'tp', scatter_dimension=1, tiled=True)  32.2 us
    all_to_all x1, waiting for transfers between devices, body(): lax.all_to_all(outgoing_slabs, 'grp', split_axis=0, concat_axis=0, tiled=...  24.6 us
    unnamed x26, local copies, waits for them, and re-layouts  19.1 us
    all_gather x1, blocking collectives, body(): whole_rows = lax.all_gather(normed, 'tp', axis=1, tiled=True)  12.7 us
    all_to_all x1, waiting for transfers between devices, body(): lax.all_to_all(outgoing, ('grp', 'tp'), split_axis=0, concat_axis=0, tile...  12.7 us
    psum x1, blocking collectives, body(): squares = lax.psum(jnp.sum(hidden_state * hidden_state, axis=1), 'tp')  12.7 us
    all_to_all x1, starting transfers between devices, body(): lax.all_to_all(outgoing, ('grp', 'tp'), split_axis=0, concat_axis=0, tile...  8.49 us
  transfers between devices with their start and end apart: 4, of which 4 were waited for; matrix products, arithmetic and copies ran while one was open for 16% of the time, Pallas kernels for 0%

commit v1 on v0

v1 whole, which is shorter than its diff:
```python
import functools

import jax
import jax.numpy as jnp
from jax import lax
from jax.experimental import pallas as pl
from jax.experimental.pallas import tpu as pltpu
from jax.sharding import PartitionSpec as P

MESH = pl.DeviceIdType.MESH
F32 = jnp.float32
BF16 = jnp.bfloat16
D = 6144
BW = 768
ROWS = 8
HEADS = 6
HD = 128
SPAN = 384
HID = 256
PIECE = 48


def remote(src, dst, send_sem, recv_sem, grp, tp):
    return pltpu.make_async_remote_copy(
        src_ref=src,
        dst_ref=dst,
        send_sem=send_sem,
        recv_sem=recv_sem,
        device_id=(grp, tp),
        device_id_type=MESH,
    )


def kernel(
    lengths,
    eids,
    gates,
    mrows,
    mdest,
    q_hbm,
    kv_hbm,
    new_hbm,
    res_hbm,
    gain_ref,
    wo_hbm,
    wi_hbm,
    wd_hbm,
    mixed,
    landed,
    q_v,
    kv_v,
    new_v,
    res_v,
    wo_v,
    wi_v,
    wd_v,
    mig_out,
    mig_mid,
    mig_out2,
    gate_buf,
    rs_send,
    rs_recv,
    hid_v,
    sq_buf,
    y_buf,
    xb,
    act_v,
    acc_v,
    r1_send,
    r1_recv,
    r2_send,
    r2_recv,
    r3_send,
    r3_recv,
    r4_send,
    r4_recv,
    in_sem,
    wo_sem,
    loc_sem,
    mig_s,
    mig_r,
    mig2_s,
    mig2_r,
    gate_s,
    gate_r,
    rs_s,
    rs_r,
    sq_s,
    sq_r,
    ag1_s,
    ag1_r,
    ag2_s,
    ag2_r,
    ag3_s,
    ag3_r,
    ag4_s,
    ag4_r,
    r1_s,
    r1_r,
    r2_s,
    r2_r,
    r3_s,
    r3_r,
    r4_s,
    r4_r,
):
    g = lax.axis_index("grp")
    t = lax.axis_index("tp")
    z, x = g // 4, g % 4
    y, c = t // 2, t % 2
    second = jnp.where(c == 0, z, x)
    first = jnp.where(c == 0, x, z)
    me = second * 4 + first

    def grp_of(sec, fst):
        return jnp.where(c == 0, sec * 4 + fst, fst * 4 + sec)

    ins = [
        pltpu.make_async_copy(kv_hbm, kv_v, in_sem.at[0]),
        pltpu.make_async_copy(q_hbm, q_v, in_sem.at[1]),
        pltpu.make_async_copy(new_hbm, new_v, in_sem.at[2]),
        pltpu.make_async_copy(res_hbm, res_v, in_sem.at[3]),
    ]
    for cp in ins:
        cp.start()

    def wo_copy(i):
        b = (t + 1 + i) % 8
        return pltpu.make_async_copy(
            wo_hbm.at[:, pl.ds(pl.multiple_of(b * BW, BW), BW)], wo_v.at[i], wo_sem.at[i]
        )

    for i in range(8):
        wo_copy(i).start()
    wi_cp = pltpu.make_async_copy(wi_hbm.reshape(2 * D, HID), wi_v, in_sem.at[4])
    wi_cp.start()
    wd_cp = pltpu.make_async_copy(wd_hbm, wd_v, in_sem.at[5])
    wd_cp.start()

    barrier = pltpu.get_barrier_semaphore()

    @pl.loop(1, 8)
    def _(i):
        pl.semaphore_signal(barrier, inc=1, device_id=(g, (t + i) % 8), device_id_type=MESH)

    @pl.loop(1, 16)
    def _(i):
        pl.semaphore_signal(barrier, inc=1, device_id=((g + i) % 16, t), device_id_type=MESH)

    for cp in ins:
        cp.wait()
    qf = q_v[...].astype(F32).reshape(HEADS * ROWS, HD)
    qb = qf.astype(BF16)
    row_of = lax.broadcasted_iota(jnp.int32, (HEADS * ROWS, 1), 0) % ROWS
    scores = jnp.zeros((HEADS * ROWS, SPAN), F32)
    for r in range(ROWS):
        part = lax.dot_general(
            qb, kv_v[r, 0:SPAN, :], (((1,), (1,)), ((), ())), preferred_element_type=F32
        )
        scores = jnp.where(row_of == r, part, scores)
    scaling = HD ** (-0.5)
    scores = scores * scaling
    newf = new_v[...].astype(F32)
    new_k = jnp.concatenate([newf[:, 0, :]] * HEADS, axis=0)
    new_val = jnp.concatenate([newf[:, 1, :]] * HEADS, axis=0)
    own = jnp.sum(qf * new_k, axis=1, keepdims=True) * scaling
    span = jnp.zeros((HEADS * ROWS, 1), jnp.int32)
    for r in range(ROWS):
        span = jnp.where(row_of == r, lengths[r], span)
    seen = lax.broadcasted_iota(jnp.int32, (HEADS * ROWS, SPAN), 1) < span
    top = jnp.maximum(
        jnp.max(jnp.where(seen, scores, -jnp.inf), axis=1, keepdims=True), own
    )
    spread = jnp.where(seen, jnp.exp(scores - top), 0.0)
    own_exp = jnp.exp(own - top)
    denom = jnp.sum(spread, axis=1, keepdims=True) + own_exp
    weights = (spread / denom).astype(BF16)
    own_w = (own_exp / denom).astype(BF16).astype(F32)
    mix = jnp.zeros((HEADS * ROWS, HD), F32)
    for r in range(ROWS):
        part = jnp.dot(weights, kv_v[r, SPAN : 2 * SPAN, :], preferred_element_type=F32)
        mix = jnp.where(row_of == r, part, mix)
    mix = mix + own_w * new_val
    heads = jnp.concatenate(
        [mix[h * ROWS : (h + 1) * ROWS] for h in range(HEADS)], axis=1
    ).astype(BF16)

    sub = lax.broadcasted_iota(jnp.int32, (ROWS, 128), 0)
    lane = lax.broadcasted_iota(jnp.int32, (ROWS, 128), 1)
    gate_rows = jnp.zeros((ROWS, 128), F32)
    for r in range(ROWS):
        for k in range(2):
            gate_rows = jnp.where(
                jnp.logical_and(sub == r, lane == eids[k, r]), gates[k, r], gate_rows
            )
    gate_buf[g] = gate_rows

    row = jnp.int32(0)
    leaves = jnp.int32(0)
    for i in range(8):
        hit = (mrows[i] >> 3) == g
        row = row + jnp.where(hit, mrows[i] & 7, 0)
        leaves = leaves + jnp.where(hit, 1, 0)
    limit = jnp.int32(0)
    fresh_k = jnp.zeros((1, HD), F32)
    fresh_v = jnp.zeros((1, HD), F32)
    for r in range(ROWS):
        limit = limit + jnp.where(row == r, lengths[r], 0)
        fresh_k = jnp.where(row == r, new_k[r : r + 1], fresh_k)
        fresh_v = jnp.where(row == r, new_val[r : r + 1], fresh_v)
    limit = jnp.where(leaves > 0, limit, -1)

    def sealed(k):
        pos = lax.broadcasted_iota(jnp.int32, (PIECE, HD), 0) + (k % 8) * PIECE
        old = kv_v[row, pl.ds(pl.multiple_of(k * PIECE, PIECE), PIECE), :].astype(F32)
        fresh = jnp.where(k < 8, fresh_k, fresh_v)
        return jnp.where(
            pos < limit, old, jnp.where(pos == limit, fresh, 0.0)
        ).astype(BF16)

    def seal_step(k, _):
        mig_out[k] = sealed(k)
        return 0

    lax.fori_loop(0, 16, seal_step, 0)
    mig_mid[g] = mig_out[g]

    pl.semaphore_wait(barrier, 22)

    def rs_copy(i):
        b = (t + 1 + i) % 8
        return remote(rs_send.at[i], rs_recv.at[t], rs_s.at[i], rs_r.at[t], g, b)

    def proj_step(i, _):
        wo_copy(i).wait()
        part = jnp.dot(heads, wo_v[i], preferred_element_type=F32)
        rs_send[i] = part.astype(BF16)
        rs_copy(i).start()
        return 0

    lax.fori_loop(0, 7, proj_step, 0)
    wo_copy(7).wait()
    attended = jnp.dot(heads, wo_v[7], preferred_element_type=F32)

    def gate_copy(i):
        return remote(
            gate_buf.at[g], gate_buf.at[g], gate_s.at[i], gate_r.at[g], (g + i) % 16, t
        )

    def mig_copy(i):
        k = (g + i) % 16
        return remote(mig_out.at[k], mig_mid.at[g], mig_s.at[i], mig_r.at[g], k, t)

    @pl.loop(1, 16)
    def _(i):
        gate_copy(i).start()
        mig_copy(i).start()

    hidden = res_v[...].astype(F32) + attended
    for i in range(1, 8):
        p = (t + i) % 8
        remote(rs_recv.at[p], rs_recv.at[p], rs_s.at[0], rs_r.at[p], g, t).wait_recv()
        hidden = hidden + rs_recv[p].astype(F32)
    hid_v[...] = hidden
    squares = jnp.sum(hidden * hidden, axis=1, keepdims=True)
    sq_buf[t] = jnp.broadcast_to(squares, (ROWS, 128))

    def sq_copy(i):
        return remote(
            sq_buf.at[t], sq_buf.at[t], sq_s.at[i], sq_r.at[t], g, (t + i) % 8
        )

    for i in range(1, 8):
        sq_copy(i).start()
    gain = gain_ref[...].astype(F32)
    scaled = hidden * gain
    ri = lax.broadcasted_iota(jnp.int32, (128, 128), 0)
    ci = lax.broadcasted_iota(jnp.int32, (128, 128), 1)
    spot = jnp.where(ri < 64, 2 * ri, 2 * ri - 127)
    shuffle = jnp.where(spot == ci, 1.0, 0.0).astype(BF16)
    stacked = jnp.concatenate(
        [scaled[:, k * 128 : (k + 1) * 128] for k in range(6)], axis=0
    ).astype(BF16)
    stacked = jnp.dot(stacked, shuffle, preferred_element_type=F32)
    y_buf[y] = jnp.concatenate(
        [stacked[k * ROWS : (k + 1) * ROWS] for k in range(6)], axis=1
    ).astype(BF16)

    def ag1_copy(i):
        q = (y + i) % 4
        return remote(
            y_buf.at[y], y_buf.at[y], ag1_s.at[i], ag1_r.at[y], g, q * 2 + c
        )

    for i in range(1, 4):
        ag1_copy(i).start()

    total = squares
    for i in range(1, 8):
        p = (t + i) % 8
        remote(sq_buf.at[p], sq_buf.at[p], sq_s.at[0], sq_r.at[p], g, t).wait_recv()
        total = total + sq_buf[p][:, 0:1]
    scale = lax.rsqrt(total / D + 1e-05)
    for i in range(4):
        p = (y + i) % 4
        if i > 0:
            remote(
                y_buf.at[p], y_buf.at[p], ag1_s.at[0], ag1_r.at[p], g, t
            ).wait_recv()
        xb[c, p, me] = (y_buf[p].astype(F32) * scale).astype(BF16)

    def ag2_copy(i):
        f = (first + i) % 4
        return remote(
            xb.at[c, :, me],
            xb.at[c, :, me],
            ag2_s.at[i],
            ag2_r.at[first],
            grp_of(second, f),
            t,
        )

    for i in range(1, 4):
        ag2_copy(i).start()

    def mig_recv(i):
        s = (g + i) % 16
        return remote(mig_mid.at[s], mig_mid.at[s], mig_s.at[0], mig_r.at[s], g, t)

    @pl.loop(1, 16)
    def _(i):
        mig_recv(i).wait_recv()

    def mig2_copy(j):
        return remote(mig_out2.at[j], landed.at[g], mig2_s.at[j], mig2_r.at[g], j, t)

    def route_step(i, _):
        j = (g + i) % 16
        src = jnp.int32(0)
        some = jnp.int32(0)
        for k in range(8):
            hit = mdest[k] == j
            src = src + jnp.where(hit, mrows[k] >> 3, 0)
            some = some + jnp.where(hit, 1, 0)
        piece = mig_mid[src].astype(F32)
        mig_out2[j] = jnp.where(some > 0, piece, 0.0).astype(BF16)

        @pl.when(i > 0)
        def _():
            mig2_copy(j).start()

        return 0

    lax.fori_loop(0, 16, route_step, 0)
    keep = pltpu.make_async_copy(mig_out2.at[g], landed.at[g], loc_sem)
    keep.start()

    for i in range(1, 4):
        f = (first + i) % 4
        slot = second * 4 + f
        remote(
            xb.at[c, :, slot], xb.at[c, :, slot], ag2_s.at[0], ag2_r.at[f], g, t
        ).wait_recv()

    def ag3_copy(i, yb):
        mine = pl.ds(second * 4, 4)
        s = (second + i) % 4
        return remote(
            xb.at[c, yb, mine],
            xb.at[c, yb, mine],
            ag3_s.at[yb, i],
            ag3_r.at[yb, second],
            grp_of(s, first),
            t,
        )

    for yb in range(4):
        for i in range(1, 4):
            ag3_copy(i, yb).start()

    partner = y * 2 + 1 - c

    def ag4_copy(yb):
        return remote(
            xb.at[c, yb], xb.at[c, yb], ag4_s.at[yb], ag4_r.at[yb], g, partner
        )

    wi_cp.wait()
    even = lax.broadcasted_iota(jnp.int32, (128, 128), 1) % 2 == 0

    def slot_of(h, zz, xx):
        return jnp.where(h == 0, zz * 4 + xx, xx * 4 + zz)

    def up_part(h, yb):
        blocks = [
            xb[h, yb, slot_of(h, k // 4, k % 4)].astype(F32) for k in range(16)
        ]
        rows = jnp.concatenate(blocks, axis=0)
        gate_lhs, up_lhs = [], []
        for k in range(6):
            v = rows[:, k * 128 : (k + 1) * 128]
            back = pltpu.roll(v, 127, 1)
            ahead = pltpu.roll(v, 1, 1)
            gate_lhs += [jnp.where(even, v, 0.0), jnp.where(even, back, 0.0)]
            up_lhs += [jnp.where(even, 0.0, ahead), jnp.where(even, 0.0, v)]
        lhs = jnp.concatenate(
            [
                jnp.concatenate(gate_lhs, axis=1).astype(BF16),
                jnp.concatenate(up_lhs, axis=1).astype(BF16),
            ],
            axis=0,
        )
        b = yb * 2 + h
        rhs = wi_v[pl.ds(pl.multiple_of(b * 2 * BW, 2 * BW), 2 * BW), :]
        acc_v[...] += jnp.dot(lhs, rhs, preferred_element_type=F32)

    acc_v[...] = jnp.zeros_like(acc_v)

    def up_step(yb, _):
        @pl.when(yb < 4)
        def _():
            for i in range(1, 4):
                s = (second + i) % 4
                theirs = pl.ds(s * 4, 4)
                remote(
                    xb.at[c, yb, theirs],
                    xb.at[c, yb, theirs],
                    ag3_s.at[yb, 0],
                    ag3_r.at[yb, s],
                    g,
                    t,
                ).wait_recv()
            ag4_copy(yb).start()
            up_part(c, yb)

        @pl.when(yb > 0)
        def _():
            old = yb - 1
            remote(
                xb.at[1 - c, old],
                xb.at[1 - c, old],
                ag4_s.at[old],
                ag4_r.at[old],
                g,
                t,
            ).wait_recv()
            up_part(1 - c, old)

        return 0

    lax.fori_loop(0, 5, up_step, 0)

    @pl.loop(1, 16)
    def _(i):
        s = (g + i) % 16
        remote(
            gate_buf.at[s], gate_buf.at[s], gate_s.at[0], gate_r.at[s], g, t
        ).wait_recv()

    gate_all = jnp.concatenate([gate_buf[k] for k in range(16)], axis=0)
    expert = g // 4
    lane_all = lax.broadcasted_iota(jnp.int32, (128, 128), 1)
    gate_col = jnp.sum(
        jnp.where(lane_all == expert, gate_all, 0.0), axis=1, keepdims=True
    )
    gate_part = acc_v[0:128, :]
    up_value = acc_v[128:256, :]
    silu = gate_part / (1.0 + jnp.exp(-gate_part))
    act_v[...] = (silu * up_value * gate_col).astype(BF16)

    wd_cp.wait()

    def down(h, yb):
        b = yb * 2 + h
        cols = pl.ds(pl.multiple_of(b * BW, BW), BW)
        return jnp.dot(act_v[...], wd_v[:, cols], preferred_element_type=F32)

    def r1_copy(yb):
        return remote(
            r1_send.at[yb], r1_recv.at[yb], r1_s.at[yb], r1_r.at[yb], g, partner
        )

    def r1_step(yb, _):
        h = 1 - c
        part = down(h, yb)
        for k in range(16):
            r1_send[yb, slot_of(h, k // 4, k % 4)] = part[
                k * ROWS : (k + 1) * ROWS
            ].astype(BF16)
        r1_copy(yb).start()
        return 0

    lax.fori_loop(0, 4, r1_step, 0)

    def r2_copy(i, yb):
        s = (second + i) % 4
        return remote(
            r2_send.at[yb, pl.ds(s * 4, 4)],
            r2_recv.at[second, yb],
            r2_s.at[yb, i],
            r2_r.at[yb, second],
            grp_of(s, first),
            t,
        )

    def r2_step(yb, _):
        part = down(c, yb)
        remote(
            r1_recv.at[yb], r1_recv.at[yb], r1_s.at[yb], r1_r.at[yb], g, t
        ).wait_recv()
        for k in range(16):
            slot = slot_of(c, k // 4, k % 4)
            both = part[k * ROWS : (k + 1) * ROWS] + r1_recv[yb, slot].astype(F32)
            r2_send[yb, slot] = both.astype(BF16)
        for i in range(1, 4):
            r2_copy(i, yb).start()
        return 0

    lax.fori_loop(0, 4, r2_step, 0)

    def r2_sum(yb, _):
        total2 = r2_send[yb, pl.ds(second * 4, 4)].astype(F32)
        for i in range(1, 4):
            s = (second + i) % 4
            remote(
                r2_recv.at[s, yb],
                r2_recv.at[s, yb],
                r2_s.at[yb, 0],
                r2_r.at[yb, s],
                g,
                t,
            ).wait_recv()
            total2 = total2 + r2_recv[s, yb].astype(F32)
        r3_send[:, yb] = total2.astype(BF16)
        return 0

    lax.fori_loop(0, 4, r2_sum, 0)

    def r3_copy(i):
        f = (first + i) % 4
        return remote(
            r3_send.at[f],
            r3_recv.at[first],
            r3_s.at[i],
            r3_r.at[first],
            grp_of(second, f),
            t,
        )

    for i in range(1, 4):
        r3_copy(i).start()
    total3 = r3_send[first].astype(F32)
    for i in range(1, 4):
        f = (first + i) % 4
        remote(
            r3_recv.at[f], r3_recv.at[f], r3_s.at[0], r3_r.at[f], g, t
        ).wait_recv()
        total3 = total3 + r3_recv[f].astype(F32)
    r4_send[...] = total3.astype(BF16)

    def r4_copy(i):
        q = (y + i) % 4
        return remote(
            r4_send.at[q], r4_recv.at[y], r4_s.at[i], r4_r.at[y], g, q * 2 + c
        )

    for i in range(1, 4):
        r4_copy(i).start()
    result = hid_v[...] + r4_send[y].astype(F32)
    for i in range(1, 4):
        q = (y + i) % 4
        remote(
            r4_recv.at[q], r4_recv.at[q], r4_s.at[0], r4_r.at[q], g, t
        ).wait_recv()
        result = result + r4_recv[q].astype(F32)
    mixed[...] = result.astype(BF16)

    keep.wait()

    @pl.loop(1, 16)
    def _(i):
        s = (g + i) % 16
        remote(
            landed.at[s], landed.at[s], mig2_s.at[0], mig2_r.at[s], g, t
        ).wait_recv()
        mig2_copy(s).wait_send()
        mig_copy(i).wait_send()
        gate_copy(i).wait_send()

    for i in range(7):
        rs_copy(i).wait_send()
        sq_copy(i + 1).wait_send()
    for i in range(1, 4):
        ag1_copy(i).wait_send()
        ag2_copy(i).wait_send()
        r3_copy(i).wait_send()
        r4_copy(i).wait_send()

    @pl.loop(0, 4)
    def _(yb):
        ag4_copy(yb).wait_send()
        r1_copy(yb).wait_send()
        for i in range(1, 4):
            ag3_copy(i, yb).wait_send()
            r2_copy(i, yb).wait_send()


def body(
    queries,
    kv_cache,
    new_kv,
    lengths,
    residual,
    w_out,
    norm_gain,
    expert_ids,
    gate_w,
    w_inner,
    w_down,
    mig_rows,
    mig_dest,
):
    vmem = pltpu.VMEM
    dma = pltpu.SemaphoreType.DMA
    smem_spec = pl.BlockSpec(memory_space=pltpu.SMEM)
    any_spec = pl.BlockSpec(memory_space=pl.ANY)
    vmem_spec = pl.BlockSpec(memory_space=pltpu.VMEM)
    mixed, landed = pl.pallas_call(
        kernel,
        out_shape=(
            jax.ShapeDtypeStruct((ROWS, BW), BF16),
            jax.ShapeDtypeStruct((16, PIECE, HD), BF16),
        ),
        in_specs=[smem_spec] * 5 + [any_spec] * 4 + [vmem_spec] + [any_spec] * 3,
        out_specs=(vmem_spec, any_spec),
        scratch_shapes=[
            vmem((HEADS, ROWS, HD), BF16),
            vmem((ROWS, 2 * SPAN, HD), BF16),
            vmem((ROWS, 2, HD), BF16),
            vmem((ROWS, BW), BF16),
            vmem((8, BW, BW), BF16),
            vmem((2 * D, HID), BF16),
            vmem((HID, D), BF16),
            vmem((16, PIECE, HD), BF16),
            vmem((16, PIECE, HD), BF16),
            vmem((16, PIECE, HD), BF16),
            vmem((16, ROWS, 128), F32),
            vmem((8, ROWS, BW), BF16),
            vmem((8, ROWS, BW), BF16),
            vmem((ROWS, BW), F32),
            vmem((8, ROWS, 128), F32),
            vmem((4, ROWS, BW), BF16),
            vmem((2, 4, 16, ROWS, BW), BF16),
            vmem((128, HID), BF16),
            vmem((256, HID), F32),
            vmem((4, 16, ROWS, BW), BF16),
            vmem((4, 16, ROWS, BW), BF16),
            vmem((4, 16, ROWS, BW), BF16),
            vmem((4, 4, 4, ROWS, BW), BF16),
            vmem((4, 4, ROWS, BW), BF16),
            vmem((4, 4, ROWS, BW), BF16),
            vmem((4, ROWS, BW), BF16),
            vmem((4, ROWS, BW), BF16),
            dma((6,)),
            dma((8,)),
            dma,
            dma((16,)),
            dma((16,)),
            dma((16,)),
            dma((16,)),
            dma((16,)),
            dma((16,)),
            dma((8,)),
            dma((8,)),
            dma((8,)),
            dma((8,)),
            dma((4,)),
            dma((4,)),
            dma((4,)),
            dma((4,)),
            dma((4, 4)),
            dma((4, 4)),
            dma((4,)),
            dma((4,)),
            dma((4,)),
            dma((4,)),
            dma((4, 4)),
            dma((4, 4)),
            dma((4,)),
            dma((4,)),
            dma((4,)),
            dma((4,)),
        ],
        compiler_params=pltpu.CompilerParams(
            collective_id=0,
            has_side_effects=True,
            vmem_limit_bytes=56 * 2**20,
        ),
        cost_estimate=pl.CostEstimate(
            flops=2 * (8 * BW * D + 256 * 2 * D * HID + 128 * HID * D),
            bytes_accessed=21 * 10**6,
            transcendentals=128 * HID,
        ),
    )(
        lengths,
        expert_ids.T,
        gate_w.T,
        mig_rows,
        mig_dest,
        queries.transpose(1, 0, 2),
        kv_cache.reshape(ROWS, 2 * SPAN, HD),
        new_kv.reshape(ROWS, 2, HD),
        residual,
        norm_gain.astype(F32).reshape(1, BW),
        w_out,
        w_inner,
        w_down,
    )
    return mixed, landed.reshape(1, 2, 1, SPAN, HD)


def solution(mesh):
    in_specs = (
        P("grp", "tp", None),
        P("grp", None, "tp", None, None),
        P("grp", None, "tp", None),
        P("grp"),
        P("grp", "tp"),
        P("tp", None),
        P("tp"),
        P("grp", None),
        P("grp", None),
        P(None, None, ("grp", "tp")),
        P(("grp", "tp"), None),
        P(),
        P(),
    )
    out_specs = (P("grp", "tp"), P("grp", None, "tp", None, None))
    return jax.shard_map(body, mesh=mesh, in_specs=in_specs, out_specs=out_specs, check_vma=False)
```

time: 227 us -> 58 us (0.26)
  waiting for transfers between devices: 106 us -> 0 us
  Pallas kernels: 0 us -> 52.9 us
  blocking collectives: 25.4 us -> 0 us
  starting transfers between devices: 18.8 us -> 0 us
  local copies, waits for them, and re-layouts: 22.5 us -> 4.19 us
  matrix products: 18.3 us -> 0 us
  between operations: 18.9 us -> 0.64 us
  other arithmetic: 15.5 us -> 0 us
    all_to_all x3 -> x0, waiting for transfers between devices: 73.7 us -> none  [the longest x1 36.4 us: body(): lax.all_to_all(down_term, ('grp', 'tp'), split_axis=0, concat_axis=0, til...]
    pallas_call x0 -> x1, Pallas kernels: none -> 52.9 us  [body(): pl.pallas_call(kernel, out_shape=(jax.ShapeDtypeStruct((ROWS, BW), BF16),...]
    reduce_scatter x1 -> x0, waiting for transfers between devices: 32.2 us -> none  [body(): lax.psum_scatter(partial_value, 'tp', scatter_dimension=1, tiled=True)]
    all_to_all x3 -> x0, starting transfers between devices: 18.8 us -> none  [the longest x1 8.49 us: body(): lax.all_to_all(outgoing, ('grp', 'tp'), split_axis=0, concat_axis=0, tile...]
    dot_general x10 -> x0, matrix products: 18.3 us -> none  [the longest x1 5.72 us: body(): jnp.dot(heads_out, w_out, preferred_element_type=jnp.float32)]
    unnamed x26 -> x2, local copies, waits for them, and re-layouts: 19.1 us -> 2.92 us
    all_gather x1 -> x0, blocking collectives: 12.7 us -> none  [body(): whole_rows = lax.all_gather(normed, 'tp', axis=1, tiled=True)]
    psum x1 -> x0, blocking collectives: 12.7 us -> none  [body(): squares = lax.psum(jnp.sum(hidden_state * hidden_state, axis=1), 'tp')]
  transfers between devices with their start and end apart: 4 -> 0, of which waited for: 4 -> 0; matrix products, arithmetic and copies ran while one was open for 16% -> 0% of each run, Pallas kernels for 0% -> 0%
where the time goes in v1:
time: 58 us; the launch traced here: 57.7 us
  Pallas kernels  52.9 us (91%)
  local copies, waits for them, and re-layouts  4.19 us (7%)
  between operations  0.64 us (1%)
    pallas_call x1, Pallas kernels, body(): pl.pallas_call(kernel, out_shape=(jax.ShapeDtypeStruct((ROWS, BW), BF16),...  52.9 us
    unnamed x2, local copies, waits for them, and re-layouts  2.92 us
    reshape x1, local copies, waits for them, and re-layouts, body(): norm_gain.astype(F32).reshape(1, BW)  1.26 us

profile of v1, /device:TPU:0, one launch (start us, length us, event | category | flops | bytes accessed | tf_op | source)
XLA Modules:
  0.0 57.7 jit_solution(956838523963448347)
XLA Ops:
  0.6 1.3 %reshape.24.gain_ref = f32[1,768]{1,0:T(1,128)} reshape(bf16[768]{0:T(1024)(128)(2,1)} %param.19) | data formatting | bytes 4608 | tf_op jit(solution)/shard_map/reshape | solution.py:714
  1.9 52.9 %shard_map.140 = (bf16[8,768]{1,0:T(8,128)(2,1)}, bf16[16,48,128]{2,1,0:T(8,128)(2,1)}) custom-call(s32[8]{0:T(128)} %lengths.1, s32[2,8]{1,0:T(2,128)} %bitcast.12, f32[2,8]{1,0:T(2,128)} %bitcast.13, s32[8]{0:T(128)} %mrows.1, s32[8]{0:T(128)} %mdest.1, bf16[6,8,128]{2,1,0:T(8,128)(2,1)} %bitcast.10, bf16[8,768,128]{2,1,0:T(8,128)(2,1)} %bitcast.8, ...), custom_call_target="tpu_custom_call" | custom-call | flops 2088763392 | bytes 21000000 | tf_op jit(solution)/shard_map/pallas_call | solution.py:628
  54.8 1.3 %copy.18 = bf16[8,768]{1,0:T(8,128)(2,1)} copy(bf16[8,768]{1,0:T(8,128)(2,1)} %get-tuple-element.10) | data formatting | bytes 24576
  56.1 1.6 %copy.19 = bf16[1,2,1,384,128]{4,3,2,1,0:T(8,128)(2,1)} copy(bf16[1,2,1,384,128]{4,3,2,1,0:T(8,128)(2,1)} %bitcast.9) | data formatting | bytes 393216

commit v2 on v1

v2 whole, which is shorter than its diff:
```python
import functools

import jax
import jax.numpy as jnp
from jax import lax
from jax.experimental import pallas as pl
from jax.experimental.pallas import tpu as pltpu
from jax.sharding import PartitionSpec as P

MESH = pl.DeviceIdType.MESH
F32 = jnp.float32
BF16 = jnp.bfloat16
D = 6144
EXPERTS = 4
BW = 768
ROWS = 8
HEADS = 6
HD = 128
SPAN = 384
HID = 256
PIECE = 48


def remote(src, dst, send_sem, recv_sem, grp, tp):
    return pltpu.make_async_remote_copy(
        src_ref=src,
        dst_ref=dst,
        send_sem=send_sem,
        recv_sem=recv_sem,
        device_id=(grp, tp),
        device_id_type=MESH,
    )


def kernel(
    len_hbm,
    eids_hbm,
    gates_hbm,
    mrows_hbm,
    mdest_hbm,
    q_hbm,
    kv_hbm,
    new_hbm,
    res_hbm,
    gain_hbm,
    wo_hbm,
    wi_hbm,
    wd_hbm,
    mixed,
    landed,
    lengths,
    eids,
    gates,
    mrows,
    mdest,
    q_v,
    kv_v,
    new_v,
    res_v,
    gain_ref,
    wo_v,
    wi_v,
    wd_v,
    mig_out,
    mig_mid,
    mig_out2,
    gate_buf,
    gain_buf,
    p_send,
    p_recv,
    sum_v,
    a_send,
    a_recv,
    hid_v,
    sq_buf,
    xb,
    act_v,
    acc_v,
    r1_send,
    r1_recv,
    r2_send,
    r2_recv,
    in_sem,
    wo_sem,
    loc_sem,
    mig_s,
    mig_r,
    mig2_s,
    mig2_r,
    gate_s,
    gate_r,
    gain_s,
    gain_r,
    p_s,
    p_r,
    a_s,
    a_r,
    sq_s,
    sq_r,
    ag_s,
    ag_r,
    agc_s,
    agc_r,
    r1_s,
    r1_r,
    r2_s,
    r2_r,
    ready,
):
    g = lax.axis_index("grp")
    t = lax.axis_index("tp")
    z, x = g // 4, g % 4
    y, c = t // 2, t % 2
    partner = y * 2 + 1 - c

    def taken(ref, sem):
        remote(ref, ref, sem, sem, g, t).wait_recv()

    def sent(ref, sem):
        remote(ref, ref, sem, sem, g, t).wait_send()

    ins = [
        pltpu.make_async_copy(kv_hbm, kv_v, in_sem.at[0]),
        pltpu.make_async_copy(q_hbm, q_v, in_sem.at[1]),
        pltpu.make_async_copy(new_hbm, new_v, in_sem.at[2]),
        pltpu.make_async_copy(res_hbm, res_v, in_sem.at[3]),
        pltpu.make_async_copy(len_hbm, lengths, in_sem.at[6]),
        pltpu.make_async_copy(eids_hbm, eids, in_sem.at[7]),
        pltpu.make_async_copy(gates_hbm, gates, in_sem.at[8]),
        pltpu.make_async_copy(mrows_hbm, mrows, in_sem.at[9]),
        pltpu.make_async_copy(mdest_hbm, mdest, in_sem.at[10]),
        pltpu.make_async_copy(gain_hbm, gain_ref, in_sem.at[11]),
    ]
    for cp in ins:
        cp.start()

    def wo_copy(i):
        b = (i % 4) * 2 + (1 - c if i < 4 else c)
        return pltpu.make_async_copy(
            wo_hbm.at[:, pl.ds(pl.multiple_of(b * BW, BW), BW)], wo_v.at[i], wo_sem.at[i]
        )

    wi_cp = pltpu.make_async_copy(wi_hbm.reshape(2 * D, HID), wi_v, in_sem.at[4])
    wd_cp = pltpu.make_async_copy(wd_hbm, wd_v, in_sem.at[5])
    for i in range(3):
        wo_copy(i).start()

    barrier = pltpu.get_barrier_semaphore()

    def greet(sem, grp, tp):
        pl.semaphore_signal(sem, inc=1, device_id=(grp, tp), device_id_type=MESH)

    greet(barrier, g, partner)
    for d in range(1, 4):
        greet(barrier, g, ((y + d) % 4) * 2 + c)
        greet(barrier, (g + 4 * d) % 16, t)
        greet(barrier, z * 4 + (x + d) % 4, t)

    for cp in ins:
        cp.wait()
    wo_copy(3).start()
    qf = q_v[...].astype(F32).reshape(HEADS * ROWS, HD)
    qb = qf.astype(BF16)
    row_of = lax.broadcasted_iota(jnp.int32, (HEADS * ROWS, 1), 0) % ROWS
    scores = jnp.zeros((HEADS * ROWS, SPAN), F32)
    for r in range(ROWS):
        part = lax.dot_general(
            qb, kv_v[r, 0:SPAN, :], (((1,), (1,)), ((), ())), preferred_element_type=F32
        )
        scores = jnp.where(row_of == r, part, scores)
    wo_copy(4).start()
    scaling = HD ** (-0.5)
    scores = scores * scaling
    newf = new_v[...].astype(F32)
    new_k = jnp.concatenate([newf[:, 0, :]] * HEADS, axis=0)
    new_val = jnp.concatenate([newf[:, 1, :]] * HEADS, axis=0)
    own = jnp.sum(qf * new_k, axis=1, keepdims=True) * scaling
    span = jnp.zeros((HEADS * ROWS, 1), jnp.int32)
    for r in range(ROWS):
        span = jnp.where(row_of == r, lengths[r], span)
    seen = lax.broadcasted_iota(jnp.int32, (HEADS * ROWS, SPAN), 1) < span
    top = jnp.maximum(
        jnp.max(jnp.where(seen, scores, -jnp.inf), axis=1, keepdims=True), own
    )
    spread = jnp.where(seen, jnp.exp(scores - top), 0.0)
    own_exp = jnp.exp(own - top)
    denom = jnp.sum(spread, axis=1, keepdims=True) + own_exp
    weights = (spread / denom).astype(BF16)
    own_w = (own_exp / denom).astype(BF16).astype(F32)
    wo_copy(5).start()
    mix = jnp.zeros((HEADS * ROWS, HD), F32)
    for r in range(ROWS):
        part = jnp.dot(weights, kv_v[r, SPAN : 2 * SPAN, :], preferred_element_type=F32)
        mix = jnp.where(row_of == r, part, mix)
    mix = mix + own_w * new_val
    heads = jnp.concatenate(
        [mix[h * ROWS : (h + 1) * ROWS] for h in range(HEADS)], axis=1
    ).astype(BF16)
    wo_copy(6).start()
    wo_copy(7).start()

    row = jnp.int32(0)
    leaves = jnp.int32(0)
    for i in range(8):
        hit = (mrows[i] >> 3) == g
        row = row + jnp.where(hit, mrows[i] & 7, 0)
        leaves = leaves + jnp.where(hit, 1, 0)
    limit = jnp.int32(0)
    fresh_k = jnp.zeros((1, HD), F32)
    fresh_v = jnp.zeros((1, HD), F32)
    for r in range(ROWS):
        limit = limit + jnp.where(row == r, lengths[r], 0)
        fresh_k = jnp.where(row == r, new_k[r : r + 1], fresh_k)
        fresh_v = jnp.where(row == r, new_val[r : r + 1], fresh_v)
    limit = jnp.where(leaves > 0, limit, -1)

    def sealed(k):
        pos = lax.broadcasted_iota(jnp.int32, (PIECE, HD), 0) + (k % 8) * PIECE
        old = kv_v[row, pl.ds(pl.multiple_of(k * PIECE, PIECE), PIECE), :].astype(F32)
        fresh = jnp.where(k < 8, fresh_k, fresh_v)
        return jnp.where(
            pos < limit, old, jnp.where(pos == limit, fresh, 0.0)
        ).astype(BF16)

    def seal_step(k, _):
        mig_out[k] = sealed(k)
        return 0

    lax.fori_loop(0, 16, seal_step, 0)
    mig_mid[g] = mig_out[g]
    gain_buf[y] = jnp.broadcast_to(
        gain_ref[...].astype(F32).reshape(1, BW), (ROWS, BW)
    ).astype(BF16)

    for i in range(4):
        wo_copy(i).wait()
        p_send[i] = jnp.dot(heads, wo_v[i], preferred_element_type=F32).astype(BF16)

    pl.semaphore_wait(barrier, 10)
    for d in range(1, 4):
        greet(ready, z * 4 + (x + d) % 4, t)

    def p_copy(i):
        return remote(p_send.at[i], p_recv.at[i], p_s, p_r.at[i], g, partner)

    def a_copy(i, d):
        q = (y + d) % 4
        return remote(a_send.at[i], a_recv.at[i, y], a_s, a_r.at[i], g, q * 2 + c)

    def gain_copy(d):
        q = (y + d) % 4
        return remote(gain_buf.at[y], gain_buf.at[y], gain_s, gain_r, g, q * 2 + c)

    def mig_copy(i):
        k = (g + i) % 16
        return remote(mig_out.at[k], mig_mid.at[g], mig_s, mig_r, k, t)

    for i in range(4):
        p_copy(i).start()
    for d in range(1, 4):
        gain_copy(d).start()
    wi_cp.start()
    wd_cp.start()
    for i in range(4):
        wo_copy(i + 4).wait()
        part = jnp.dot(heads, wo_v[i + 4], preferred_element_type=F32)
        taken(p_recv.at[i], p_r.at[i])
        part = part + p_recv[i].astype(F32)
        part = part + jnp.where(y == i, res_v[...].astype(F32), 0.0)
        sum_v[i] = part
        a_send[i] = part.astype(BF16)
        for d in range(1, 4):
            a_copy(i, d).start()

    pl.semaphore_wait(ready, 3)

    @pl.loop(1, 16)
    def _(i):
        mig_copy(i).start()

    sub = lax.broadcasted_iota(jnp.int32, (ROWS, 128), 0)
    lane = lax.broadcasted_iota(jnp.int32, (ROWS, 128), 1)
    gate_rows = jnp.zeros((ROWS, 128), F32)
    for r in range(ROWS):
        for k in range(2):
            gate_rows = jnp.where(
                jnp.logical_and(sub == r, lane == eids[k, r]), gates[k, r], gate_rows
            )

    ri = lax.broadcasted_iota(jnp.int32, (128, 128), 0)
    ci = lax.broadcasted_iota(jnp.int32, (128, 128), 1)
    spot = jnp.where(ri < 64, 2 * ri, 2 * ri - 127)
    shuffle = jnp.where(spot == ci, 1.0, 0.0).astype(BF16)

    def ag_copy(i, d):
        return remote(
            xb.at[c, i, g], xb.at[c, i, g], ag_s, ag_r.at[i], (g + d) % 16, t
        )

    taken(gain_buf.at[pl.ds(0, 3)], gain_r)
    squares = jnp.zeros((ROWS, 1), F32)
    for i in range(4):
        taken(a_recv.at[i, pl.ds(0, 3)], a_r.at[i])
        hidden = sum_v[i]
        for d in range(1, 4):
            hidden = hidden + a_recv[i, (y + d) % 4].astype(F32)
        hid_v[i] = hidden
        squares = squares + jnp.sum(hidden * hidden, axis=1, keepdims=True)
        scaled = hidden * gain_buf[i].astype(F32)
        stacked = jnp.concatenate(
            [scaled[:, k * 128 : (k + 1) * 128] for k in range(6)], axis=0
        ).astype(BF16)
        stacked = jnp.dot(stacked, shuffle, preferred_element_type=F32)
        xb[c, i, g] = jnp.concatenate(
            [stacked[k * ROWS : (k + 1) * ROWS] for k in range(6)], axis=1
        ).astype(BF16)

        @pl.loop(1, 16)
        def _(d):
            ag_copy(i, d).start()

    sq_buf[0] = jnp.broadcast_to(squares, (ROWS, 128))
    sq_copy = remote(sq_buf.at[0], sq_buf.at[1], sq_s, sq_r, g, partner)
    sq_copy.start()
    taken(sq_buf.at[1], sq_r)
    scale = lax.rsqrt((sq_buf[0] + sq_buf[1]) / D + 1e-05)
    gate_buf[g] = jnp.where(lane == EXPERTS, scale, gate_rows)

    def gate_copy(i):
        return remote(
            gate_buf.at[g], gate_buf.at[g], gate_s, gate_r, (g + i) % 16, t
        )

    @pl.loop(1, 16)
    def _(i):
        gate_copy(i).start()

    taken(mig_mid.at[pl.ds(0, 15)], mig_r)

    def mig2_copy(j):
        return remote(mig_out2.at[j], landed.at[g], mig2_s, mig2_r, j, t)

    def route_step(i, _):
        j = (g + i) % 16
        src = jnp.int32(0)
        some = jnp.int32(0)
        for k in range(8):
            hit = mdest[k] == j
            src = src + jnp.where(hit, mrows[k] >> 3, 0)
            some = some + jnp.where(hit, 1, 0)
        piece = mig_mid[src].astype(F32)
        mig_out2[j] = jnp.where(some > 0, piece, 0.0).astype(BF16)

        @pl.when(i > 0)
        def _():
            mig2_copy(j).start()

        return 0

    lax.fori_loop(0, 16, route_step, 0)
    keep = pltpu.make_async_copy(mig_out2.at[g], landed.at[g], loc_sem)
    keep.start()

    sent(p_send, p_s)
    sent(a_recv.at[pl.ds(0, 3)], a_s)
    sent(gain_buf.at[pl.ds(0, 3)], gain_s)
    sent(mig_out.at[pl.ds(0, 15)], mig_s)
    sent(sq_buf.at[0], sq_s)

    wi_cp.wait()
    even = lax.broadcasted_iota(jnp.int32, (128, 128), 1) % 2 == 0

    def agc_copy(i):
        return remote(xb.at[c, i], xb.at[c, i], agc_s, agc_r.at[i], g, partner)

    def up_part(h, yb):
        rows = jnp.concatenate(
            [xb[h, yb, k].astype(F32) for k in range(16)], axis=0
        )
        gate_lhs, up_lhs = [], []
        for k in range(6):
            v = rows[:, k * 128 : (k + 1) * 128]
            back = pltpu.roll(v, 127, 1)
            ahead = pltpu.roll(v, 1, 1)
            gate_lhs += [jnp.where(even, v, 0.0), jnp.where(even, back, 0.0)]
            up_lhs += [jnp.where(even, 0.0, ahead), jnp.where(even, 0.0, v)]
        lhs = jnp.concatenate(
            [
                jnp.concatenate(gate_lhs, axis=1).astype(BF16),
                jnp.concatenate(up_lhs, axis=1).astype(BF16),
            ],
            axis=0,
        )
        b = yb * 2 + h
        rhs = wi_v[pl.ds(pl.multiple_of(b * 2 * BW, 2 * BW), 2 * BW), :]
        acc_v[...] += jnp.dot(lhs, rhs, preferred_element_type=F32)

    acc_v[...] = jnp.zeros_like(acc_v)

    def up_step(yb, _):
        @pl.when(yb < 4)
        def _():
            taken(xb.at[c, yb, pl.ds(0, 15)], ag_r.at[yb])
            agc_copy(yb).start()
            up_part(c, yb)

        @pl.when(yb > 0)
        def _():
            taken(xb.at[1 - c, yb - 1], agc_r.at[yb - 1])
            up_part(1 - c, yb - 1)

        return 0

    lax.fori_loop(0, 5, up_step, 0)

    taken(gate_buf.at[pl.ds(0, 15)], gate_r)
    gate_all = jnp.concatenate([gate_buf[k] for k in range(16)], axis=0)
    expert = g // 4
    lane_all = lax.broadcasted_iota(jnp.int32, (128, 128), 1)
    gate_col = jnp.sum(
        jnp.where(lane_all == expert, gate_all, 0.0), axis=1, keepdims=True
    )
    scale_col = gate_all[:, EXPERTS : EXPERTS + 1]
    gate_part = acc_v[0:128, :] * scale_col
    up_value = acc_v[128:256, :] * scale_col
    silu = gate_part / (1.0 + jnp.exp(-gate_part))
    act_v[...] = (silu * up_value * gate_col).astype(BF16)

    wd_cp.wait()

    def down(h, yb):
        b = yb * 2 + h
        cols = pl.ds(pl.multiple_of(b * BW, BW), BW)
        return jnp.dot(act_v[...], wd_v[:, cols], preferred_element_type=F32)

    def r1_copy(yb):
        return remote(r1_send.at[yb], r1_recv.at[yb], r1_s, r1_r.at[yb], g, partner)

    def r1_step(j, _):
        yb = (y + 1 + j) % 4
        part = down(1 - c, yb)
        for k in range(16):
            r1_send[yb, k] = part[k * ROWS : (k + 1) * ROWS].astype(BF16)
        r1_copy(yb).start()
        return 0

    lax.fori_loop(0, 4, r1_step, 0)

    def r2_copy(j, yb, k):
        return remote(
            r2_send.at[yb, k], r2_recv.at[y, g], r2_s.at[j // 3], r2_r.at[y], k, yb * 2 + c
        )

    def r2_step(j, _):
        yb = (y + 1 + j) % 4
        part = down(c, yb)
        taken(r1_recv.at[yb], r1_r.at[yb])
        for k in range(16):
            both = part[k * ROWS : (k + 1) * ROWS] + r1_recv[yb, k].astype(F32)
            r2_send[yb, k] = both.astype(BF16)

        @pl.loop(1, 16)
        def _(i):
            r2_copy(j, yb, (g + i) % 16).start()

        @pl.when(j < 3)
        def _():
            r2_copy(j, yb, g).start()

        return 0

    lax.fori_loop(0, 4, r2_step, 0)

    keep.wait()
    taken(landed.at[pl.ds(0, 15)], mig2_r)
    sent(mig_out2.at[pl.ds(0, 15)], mig2_s)
    sent(gate_buf.at[pl.ds(0, 15)], gate_s)
    sent(xb.at[0, :, pl.ds(0, 15)], ag_s)
    sent(xb.at[0], agc_s)
    sent(r1_send, r1_s)

    result = hid_v[y] + r2_send[y, g].astype(F32)

    def add_from(s, first_g, count, total):
        def step(i, acc):
            return acc + r2_recv[s, (g + first_g + i) % 16].astype(F32)

        return lax.fori_loop(0, count, step, total, unroll=True)

    for j in range(3):
        s = (y + 3 - j) % 4
        taken(r2_recv.at[s], r2_r.at[s])
        result = add_from(s, 0, 16, result)
    taken(r2_recv.at[y, pl.ds(0, 15)], r2_r.at[y])
    result = add_from(y, 1, 15, result)
    mixed[...] = result.astype(BF16)
    sent(r2_send.at[pl.ds(0, 3)], r2_s.at[0])
    sent(r2_send.at[0, pl.ds(0, 15)], r2_s.at[1])


def finish(mixed_in, landed_in, mixed_out, landed_out, mixed_v, landed_v, sem):
    quarters = [pl.ds(4 * i, 4) for i in range(4)]
    into = [pltpu.make_async_copy(mixed_in, mixed_v, sem.at[4])] + [
        pltpu.make_async_copy(landed_in.at[q], landed_v.at[q], sem.at[i])
        for i, q in enumerate(quarters)
    ]
    out = [pltpu.make_async_copy(mixed_v, mixed_out, sem.at[4])] + [
        pltpu.make_async_copy(landed_v.at[q], landed_out.at[q], sem.at[i])
        for i, q in enumerate(quarters)
    ]
    for cp in into:
        cp.start()
    for first, then in zip(into, out):
        first.wait()
        then.start()
    for cp in out:
        cp.wait()


def body(
    queries,
    kv_cache,
    new_kv,
    lengths,
    residual,
    w_out,
    norm_gain,
    expert_ids,
    gate_w,
    w_inner,
    w_down,
    mig_rows,
    mig_dest,
):
    vmem = pltpu.VMEM
    dma = pltpu.SemaphoreType.DMA
    smem = pltpu.SMEM
    any_spec = pl.BlockSpec(memory_space=pl.ANY)
    vmem_spec = pl.BlockSpec(memory_space=pltpu.VMEM)
    mixed, landed = pl.pallas_call(
        kernel,
        out_shape=(
            jax.ShapeDtypeStruct((ROWS, BW), BF16),
            jax.ShapeDtypeStruct((16, PIECE, HD), BF16),
        ),
        in_specs=[any_spec] * 13,
        out_specs=(vmem_spec, any_spec),
        scratch_shapes=[
            smem((ROWS,), jnp.int32),
            smem((2, ROWS), jnp.int32),
            smem((2, ROWS), F32),
            smem((8,), jnp.int32),
            smem((8,), jnp.int32),
            vmem((HEADS, ROWS, HD), BF16),
            vmem((ROWS, 2 * SPAN, HD), BF16),
            vmem((ROWS, 2, HD), BF16),
            vmem((ROWS, BW), BF16),
            vmem((BW,), BF16),
            vmem((8, BW, BW), BF16),
            vmem((2 * D, HID), BF16),
            vmem((HID, D), BF16),
            vmem((16, PIECE, HD), BF16),
            vmem((16, PIECE, HD), BF16),
            vmem((16, PIECE, HD), BF16),
            vmem((16, ROWS, 128), F32),
            vmem((4, ROWS, BW), BF16),
            vmem((4, ROWS, BW), BF16),
            vmem((4, ROWS, BW), BF16),
            vmem((4, ROWS, BW), F32),
            vmem((4, ROWS, BW), BF16),
            vmem((4, 4, ROWS, BW), BF16),
            vmem((4, ROWS, BW), F32),
            vmem((2, ROWS, 128), F32),
            vmem((2, 4, 16, ROWS, BW), BF16),
            vmem((128, HID), BF16),
            vmem((256, HID), F32),
            vmem((4, 16, ROWS, BW), BF16),
            vmem((4, 16, ROWS, BW), BF16),
            vmem((4, 16, ROWS, BW), BF16),
            vmem((4, 16, ROWS, BW), BF16),
            dma((12,)),
            dma((8,)),
            dma,
            dma,
            dma,
            dma,
            dma,
            dma,
            dma,
            dma,
            dma,
            dma,
            dma((4,)),
            dma,
            dma((4,)),
            dma,
            dma,
            dma,
            dma((4,)),
            dma,
            dma((4,)),
            dma,
            dma((4,)),
            dma((2,)),
            dma((4,)),
            pltpu.SemaphoreType.REGULAR,
        ],
        compiler_params=pltpu.CompilerParams(
            collective_id=0,
            has_side_effects=True,
            vmem_limit_bytes=56 * 2**20,
        ),
        cost_estimate=pl.CostEstimate(
            flops=2 * (8 * BW * D + 256 * 2 * D * HID + 128 * HID * D),
            bytes_accessed=21 * 10**6,
            transcendentals=128 * HID,
        ),
    )(
        lengths,
        expert_ids.T,
        gate_w.T,
        mig_rows,
        mig_dest,
        queries.transpose(1, 0, 2),
        kv_cache.reshape(ROWS, 2 * SPAN, HD),
        new_kv.reshape(ROWS, 2, HD),
        residual,
        norm_gain,
        w_out,
        w_inner,
        w_down,
    )
    mixed, landed = pl.pallas_call(
        finish,
        out_shape=(
            jax.ShapeDtypeStruct((ROWS, BW), BF16),
            jax.ShapeDtypeStruct((16, PIECE, HD), BF16),
        ),
        in_specs=[any_spec] * 2,
        out_specs=(any_spec, any_spec),
        scratch_shapes=[
            vmem((ROWS, BW), BF16),
            vmem((16, PIECE, HD), BF16),
            dma((5,)),
        ],
        compiler_params=pltpu.CompilerParams(vmem_limit_bytes=56 * 2**20),
    )(mixed, landed)
    return mixed, landed.reshape(1, 2, 1, SPAN, HD)


def solution(mesh):
    in_specs = (
        P("grp", "tp", None),
        P("grp", None, "tp", None, None),
        P("grp", None, "tp", None),
        P("grp"),
        P("grp", "tp"),
        P("tp", None),
        P("tp"),
        P("grp", None),
        P("grp", None),
        P(None, None, ("grp", "tp")),
        P(("grp", "tp"), None),
        P(),
        P(),
    )
    out_specs = (P("grp", "tp"), P("grp", None, "tp", None, None))
    return jax.shard_map(body, mesh=mesh, in_specs=in_specs, out_specs=out_specs, check_vma=False)
```

time: 58 us -> 45.5 us (0.78)
  Pallas kernels: 52.9 us -> 44.5 us
  local copies, waits for them, and re-layouts: 4.19 us -> 0 us
    pallas_call x1, Pallas kernels: 52.9 us -> 42.9 us  [body(): pl.pallas_call(kernel, out_shape=(jax.ShapeDtypeStruct((ROWS, BW), BF16),...]
    unnamed x2 -> x0, local copies, waits for them, and re-layouts: 2.92 us -> none
    pallas_call x0 -> x1, Pallas kernels: none -> 1.55 us  [body(): pl.pallas_call(finish, out_shape=(jax.ShapeDtypeStruct((ROWS, BW), BF16),...]
    reshape x1 -> x0, local copies, waits for them, and re-layouts: 1.26 us -> none  [body(): norm_gain.astype(F32).reshape(1, BW)]
where the time goes in v2:
time: 45.5 us; the launch traced here: 45.1 us
  Pallas kernels  44.5 us (98%)
  between operations  0.64 us (1%)
    pallas_call x1, Pallas kernels, body(): pl.pallas_call(kernel, out_shape=(jax.ShapeDtypeStruct((ROWS, BW), BF16),...  42.9 us
    pallas_call x1, Pallas kernels, body(): pl.pallas_call(finish, out_shape=(jax.ShapeDtypeStruct((ROWS, BW), BF16),...  1.55 us

profile of v2, /device:TPU:0, one launch (start us, length us, event | category | flops | bytes accessed | tf_op | source)
XLA Modules:
  0.0 45.1 jit_solution(8293863274201247056)
XLA Ops:
  0.6 42.9 %shard_map.140 = (bf16[8,768]{1,0:T(8,128)(2,1)}, bf16[16,48,128]{2,1,0:T(8,128)(2,1)}) custom-call(s32[8]{0:T(128)} %len_hbm.1, s32[2,8]{1,0:T(2,128)} %bitcast.11, f32[2,8]{1,0:T(2,128)} %bitcast.12, s32[8]{0:T(128)} %mrows_hbm.1, s32[8]{0:T(128)} %mdest_hbm.1, bf16[6,8,128]{2,1,0:T(8,128)(2,1)} %bitcast.9, bf16[8,768,128]{2,1,0:T(8,128)(2,1)} %bitcast.8, ...), custom_call_target="tpu_custom_call" | custom-call | flops 2088763392 | bytes 21000000 | tf_op jit(solution)/shard_map/pallas_call | solution.py:540
  43.6 1.5 %shard_map.141 = (bf16[8,768]{1,0:T(8,128)(2,1)}, bf16[16,48,128]{2,1,0:T(8,128)(2,1)}) custom-call(bf16[8,768]{1,0:T(8,128)(2,1)} %get-tuple-element.6.mixed_in, bf16[16,48,128]{2,1,0:T(8,128)(2,1)} %get-tuple-element.7.landed_in), custom_call_target="tpu_custom_call" | custom-call | tf_op jit(solution)/shard_map/pallas_call | solution.py:633

commit v3 on v2

--- a/solution.py
+++ b/solution.py
@@ -60,14 +60,13 @@
     gain_ref,
     wo_v,
     wi_v,
+    wi2_v,
     wd_v,
     mig_out,
     mig_mid,
     mig_out2,
     gate_buf,
     gain_buf,
-    p_send,
-    p_recv,
     sum_v,
     a_send,
     a_recv,
@@ -91,8 +90,6 @@
     gate_r,
     gain_s,
     gain_r,
-    p_s,
-    p_r,
     a_s,
     a_r,
     sq_s,
@@ -135,7 +132,7 @@
         cp.start()
 
     def wo_copy(i):
-        b = (i % 4) * 2 + (1 - c if i < 4 else c)
+        b = (i // 2) * 2 + (c if i % 2 == 0 else 1 - c)
         return pltpu.make_async_copy(
             wo_hbm.at[:, pl.ds(pl.multiple_of(b * BW, BW), BW)], wo_v.at[i], wo_sem.at[i]
         )
@@ -150,9 +147,9 @@
     def greet(sem, grp, tp):
         pl.semaphore_signal(sem, inc=1, device_id=(grp, tp), device_id_type=MESH)
 
-    greet(barrier, g, partner)
+    for d in range(1, 8):
+        greet(barrier, g, (t + d) % 8)
     for d in range(1, 4):
-        greet(barrier, g, ((y + d) % 4) * 2 + c)
         greet(barrier, (g + 4 * d) % 16, t)
         greet(barrier, z * 4 + (x + d) % 4, t)
 
@@ -198,6 +195,8 @@
     ).astype(BF16)
     wo_copy(6).start()
     wo_copy(7).start()
+    wi_cp.start()
+    wd_cp.start()
 
     row = jnp.int32(0)
     leaves = jnp.int32(0)
@@ -228,24 +227,16 @@
 
     lax.fori_loop(0, 16, seal_step, 0)
     mig_mid[g] = mig_out[g]
-    gain_buf[y] = jnp.broadcast_to(
-        gain_ref[...].astype(F32).reshape(1, BW), (ROWS, BW)
-    ).astype(BF16)
-
-    for i in range(4):
-        wo_copy(i).wait()
-        p_send[i] = jnp.dot(heads, wo_v[i], preferred_element_type=F32).astype(BF16)
-
-    pl.semaphore_wait(barrier, 10)
-    for d in range(1, 4):
-        greet(ready, z * 4 + (x + d) % 4, t)
-
-    def p_copy(i):
-        return remote(p_send.at[i], p_recv.at[i], p_s, p_r.at[i], g, partner)
-
-    def a_copy(i, d):
-        q = (y + d) % 4
-        return remote(a_send.at[i], a_recv.at[i, y], a_s, a_r.at[i], g, q * 2 + c)
+    gain_buf[y] = gain_ref[...].astype(F32).reshape(1, BW)
+
+    def a_copy(i, j, d):
+        q = ((y + d) % 4) * 2 + (c if j == 0 else 1 - c)
+        return remote(a_send.at[i, j], a_recv.at[i, t], a_s, a_r.at[i], g, q)
+
+    def a_start(i):
+        for j in range(2):
+            for d in range(1 - j, 4):
+                a_copy(i, j, d).start()
 
     def gain_copy(d):
         q = (y + d) % 4
@@ -255,22 +246,29 @@
         k = (g + i) % 16
         return remote(mig_out.at[k], mig_mid.at[g], mig_s, mig_r, k, t)
 
-    for i in range(4):
-        p_copy(i).start()
+    def project(i):
+        wo_copy(2 * i).wait()
+        part = jnp.dot(heads, wo_v[2 * i], preferred_element_type=F32)
+        part = part + jnp.where(y == i, res_v[...].astype(F32), 0.0)
+        sum_v[i] = part
+        a_send[i, 0] = part.astype(BF16)
+        wo_copy(2 * i + 1).wait()
+        part = jnp.dot(heads, wo_v[2 * i + 1], preferred_element_type=F32)
+        a_send[i, 1] = part.astype(BF16)
+
+    project(0)
+    project(1)
+    pl.semaphore_wait(barrier, 13)
+    a_start(0)
+    for d in range(1, 4):
+        greet(ready, z * 4 + (x + d) % 4, t)
     for d in range(1, 4):
         gain_copy(d).start()
-    wi_cp.start()
-    wd_cp.start()
-    for i in range(4):
-        wo_copy(i + 4).wait()
-        part = jnp.dot(heads, wo_v[i + 4], preferred_element_type=F32)
-        taken(p_recv.at[i], p_r.at[i])
-        part = part + p_recv[i].astype(F32)
-        part = part + jnp.where(y == i, res_v[...].astype(F32), 0.0)
-        sum_v[i] = part
-        a_send[i] = part.astype(BF16)
-        for d in range(1, 4):
-            a_copy(i, d).start()
+    a_start(1)
+    project(2)
+    a_start(2)
+    project(3)
+    a_start(3)
 
     pl.semaphore_wait(ready, 3)
 
@@ -287,11 +285,6 @@
                 jnp.logical_and(sub == r, lane == eids[k, r]), gates[k, r], gate_rows
             )
 
-    ri = lax.broadcasted_iota(jnp.int32, (128, 128), 0)
-    ci = lax.broadcasted_iota(jnp.int32, (128, 128), 1)
-    spot = jnp.where(ri < 64, 2 * ri, 2 * ri - 127)
-    shuffle = jnp.where(spot == ci, 1.0, 0.0).astype(BF16)
-
     def ag_copy(i, d):
         return remote(
             xb.at[c, i, g], xb.at[c, i, g], ag_s, ag_r.at[i], (g + d) % 16, t
@@ -300,20 +293,13 @@
     taken(gain_buf.at[pl.ds(0, 3)], gain_r)
     squares = jnp.zeros((ROWS, 1), F32)
     for i in range(4):
-        taken(a_recv.at[i, pl.ds(0, 3)], a_r.at[i])
+        taken(a_recv.at[i, pl.ds(0, 7)], a_r.at[i])
         hidden = sum_v[i]
-        for d in range(1, 4):
-            hidden = hidden + a_recv[i, (y + d) % 4].astype(F32)
+        for d in range(1, 8):
+            hidden = hidden + a_recv[i, (t + d) % 8].astype(F32)
         hid_v[i] = hidden
         squares = squares + jnp.sum(hidden * hidden, axis=1, keepdims=True)
-        scaled = hidden * gain_buf[i].astype(F32)
-        stacked = jnp.concatenate(
-            [scaled[:, k * 128 : (k + 1) * 128] for k in range(6)], axis=0
-        ).astype(BF16)
-        stacked = jnp.dot(stacked, shuffle, preferred_element_type=F32)
-        xb[c, i, g] = jnp.concatenate(
-            [stacked[k * ROWS : (k + 1) * ROWS] for k in range(6)], axis=1
-        ).astype(BF16)
+        xb[c, i, g] = (hidden * gain_buf[i]).astype(BF16)
 
         @pl.loop(1, 16)
         def _(d):
@@ -350,25 +336,32 @@
             some = some + jnp.where(hit, 1, 0)
         piece = mig_mid[src].astype(F32)
         mig_out2[j] = jnp.where(some > 0, piece, 0.0).astype(BF16)
-
-        @pl.when(i > 0)
-        def _():
-            mig2_copy(j).start()
-
         return 0
 
     lax.fori_loop(0, 16, route_step, 0)
     keep = pltpu.make_async_copy(mig_out2.at[g], landed.at[g], loc_sem)
     keep.start()
 
-    sent(p_send, p_s)
-    sent(a_recv.at[pl.ds(0, 3)], a_s)
+    sent(a_recv.at[:, pl.ds(0, 7)], a_s)
     sent(gain_buf.at[pl.ds(0, 3)], gain_s)
     sent(mig_out.at[pl.ds(0, 15)], mig_s)
     sent(sq_buf.at[0], sq_s)
 
     wi_cp.wait()
-    even = lax.broadcasted_iota(jnp.int32, (128, 128), 1) % 2 == 0
+    ri = lax.broadcasted_iota(jnp.int32, (256, 256), 0)
+    ci = lax.broadcasted_iota(jnp.int32, (256, 256), 1)
+    spot = jnp.where(ri < 128, 2 * ri, 2 * ri - 255)
+    apart = jnp.where(spot == ci, 1.0, 0.0).astype(BF16)
+
+    def apart_step(k, _):
+        pairs = wi_v[pl.ds(pl.multiple_of(k * 256, 256), 256), :]
+        rows = jnp.dot(apart, pairs, preferred_element_type=F32).astype(BF16)
+        at = pl.ds(pl.multiple_of(k * 128, 128), 128)
+        wi2_v[at, 0:HID] = rows[0:128]
+        wi2_v[at, HID : 2 * HID] = rows[128:256]
+        return 0
+
+    lax.fori_loop(0, D // 128, apart_step, 0, unroll=4)
 
     def agc_copy(i):
         return remote(xb.at[c, i], xb.at[c, i], agc_s, agc_r.at[i], g, partner)
@@ -377,23 +370,9 @@
         rows = jnp.concatenate(
             [xb[h, yb, k].astype(F32) for k in range(16)], axis=0
         )
-        gate_lhs, up_lhs = [], []
-        for k in range(6):
-            v = rows[:, k * 128 : (k + 1) * 128]
-            back = pltpu.roll(v, 127, 1)
-            ahead = pltpu.roll(v, 1, 1)
-            gate_lhs += [jnp.where(even, v, 0.0), jnp.where(even, back, 0.0)]
-            up_lhs += [jnp.where(even, 0.0, ahead), jnp.where(even, 0.0, v)]
-        lhs = jnp.concatenate(
-            [
-                jnp.concatenate(gate_lhs, axis=1).astype(BF16),
-                jnp.concatenate(up_lhs, axis=1).astype(BF16),
-            ],
-            axis=0,
-        )
         b = yb * 2 + h
-        rhs = wi_v[pl.ds(pl.multiple_of(b * 2 * BW, 2 * BW), 2 * BW), :]
-        acc_v[...] += jnp.dot(lhs, rhs, preferred_element_type=F32)
+        rhs = wi2_v[pl.ds(pl.multiple_of(b * BW, BW), BW), :]
+        acc_v[...] += jnp.dot(rows.astype(BF16), rhs, preferred_element_type=F32)
 
     acc_v[...] = jnp.zeros_like(acc_v)
 
@@ -403,6 +382,12 @@
             taken(xb.at[c, yb, pl.ds(0, 15)], ag_r.at[yb])
             agc_copy(yb).start()
             up_part(c, yb)
+
+        @pl.when(yb == 4)
+        def _():
+            @pl.loop(1, 16)
+            def _(i):
+                mig2_copy((g + i) % 16).start()
 
         @pl.when(yb > 0)
         def _():
@@ -421,8 +406,8 @@
         jnp.where(lane_all == expert, gate_all, 0.0), axis=1, keepdims=True
     )
     scale_col = gate_all[:, EXPERTS : EXPERTS + 1]
-    gate_part = acc_v[0:128, :] * scale_col
-    up_value = acc_v[128:256, :] * scale_col
+    gate_part = acc_v[:, 0:HID] * scale_col
+    up_value = acc_v[:, HID : 2 * HID] * scale_col
     silu = gate_part / (1.0 + jnp.exp(-gate_part))
     act_v[...] = (silu * up_value * gate_col).astype(BF16)
 
@@ -498,22 +483,14 @@
     sent(r2_send.at[0, pl.ds(0, 15)], r2_s.at[1])
 
 
-def finish(mixed_in, landed_in, mixed_out, landed_out, mixed_v, landed_v, sem):
-    quarters = [pl.ds(4 * i, 4) for i in range(4)]
-    into = [pltpu.make_async_copy(mixed_in, mixed_v, sem.at[4])] + [
-        pltpu.make_async_copy(landed_in.at[q], landed_v.at[q], sem.at[i])
-        for i, q in enumerate(quarters)
+def finish(mixed_in, landed_in, mixed_out, landed_out, sem):
+    cps = [
+        pltpu.make_async_copy(mixed_in, mixed_out, sem.at[0]),
+        pltpu.make_async_copy(landed_in, landed_out, sem.at[1]),
     ]
-    out = [pltpu.make_async_copy(mixed_v, mixed_out, sem.at[4])] + [
-        pltpu.make_async_copy(landed_v.at[q], landed_out.at[q], sem.at[i])
-        for i, q in enumerate(quarters)
-    ]
-    for cp in into:
+    for cp in cps:
         cp.start()
-    for first, then in zip(into, out):
-        first.wait()
-        then.start()
-    for cp in out:
+    for cp in cps:
         cp.wait()
 
 
@@ -540,11 +517,11 @@
     mixed, landed = pl.pallas_call(
         kernel,
         out_shape=(
-            jax.ShapeDtypeStruct((ROWS, BW), BF16),
-            jax.ShapeDtypeStruct((16, PIECE, HD), BF16),
+            pltpu.VMEM((ROWS, BW), BF16),
+            pltpu.VMEM((16, PIECE, HD), BF16),
         ),
         in_specs=[any_spec] * 13,
-        out_specs=(vmem_spec, any_spec),
+        out_specs=(vmem_spec, vmem_spec),
         scratch_shapes=[
             smem((ROWS,), jnp.int32),
             smem((2, ROWS), jnp.int32),
@@ -558,22 +535,21 @@
             vmem((BW,), BF16),
             vmem((8, BW, BW), BF16),
             vmem((2 * D, HID), BF16),
+            vmem((D, 2 * HID), BF16),
             vmem((HID, D), BF16),
             vmem((16, PIECE, HD), BF16),
             vmem((16, PIECE, HD), BF16),
             vmem((16, PIECE, HD), BF16),
             vmem((16, ROWS, 128), F32),
-            vmem((4, ROWS, BW), BF16),
-            vmem((4, ROWS, BW), BF16),
-            vmem((4, ROWS, BW), BF16),
+            vmem((4, 1, BW), F32),
             vmem((4, ROWS, BW), F32),
-            vmem((4, ROWS, BW), BF16),
-            vmem((4, 4, ROWS, BW), BF16),
+            vmem((4, 2, ROWS, BW), BF16),
+            vmem((4, 8, ROWS, BW), BF16),
             vmem((4, ROWS, BW), F32),
             vmem((2, ROWS, 128), F32),
             vmem((2, 4, 16, ROWS, BW), BF16),
             vmem((128, HID), BF16),
-            vmem((256, HID), F32),
+            vmem((128, 2 * HID), F32),
             vmem((4, 16, ROWS, BW), BF16),
             vmem((4, 16, ROWS, BW), BF16),
             vmem((4, 16, ROWS, BW), BF16),
@@ -589,8 +565,6 @@
             dma,
             dma,
             dma,
-            dma,
-            dma((4,)),
             dma,
             dma((4,)),
             dma,
@@ -636,15 +610,14 @@
             jax.ShapeDtypeStruct((ROWS, BW), BF16),
             jax.ShapeDtypeStruct((16, PIECE, HD), BF16),
         ),
-        in_specs=[any_spec] * 2,
+        in_specs=[vmem_spec] * 2,
         out_specs=(any_spec, any_spec),
-        scratch_shapes=[
-            vmem((ROWS, BW), BF16),
-            vmem((16, PIECE, HD), BF16),
-            dma((5,)),
-        ],
+        scratch_shapes=[dma((2,))],
         compiler_params=pltpu.CompilerParams(vmem_limit_bytes=56 * 2**20),
-    )(mixed, landed)
+    )(
+        pltpu.with_memory_space_constraint(mixed, pltpu.VMEM),
+        pltpu.with_memory_space_constraint(landed, pltpu.VMEM),
+    )
     return mixed, landed.reshape(1, 2, 1, SPAN, HD)
 
 

time: 45.5 us -> 43.4 us (0.954)
  Pallas kernels: 44.5 us -> 42.5 us
    pallas_call x1, Pallas kernels: 42.9 us -> 41.8 us  [body(): pl.pallas_call(kernel, out_shape=(pltpu.VMEM((ROWS, BW), BF16), pltpu.VME...]
    pallas_call x1, Pallas kernels: 1.55 us -> 0.7 us  [body(): pl.pallas_call(finish, out_shape=(jax.ShapeDtypeStruct((ROWS, BW), BF16),...]
where the time goes in v3:
time: 43.4 us; the launch traced here: 43.2 us
  Pallas kernels  42.5 us (98%)
  between operations  0.64 us (1%)
    pallas_call x1, Pallas kernels, body(): pl.pallas_call(kernel, out_shape=(pltpu.VMEM((ROWS, BW), BF16), pltpu.VME...  41.8 us

profile of v3, /device:TPU:0, one launch (start us, length us, event | category | flops | bytes accessed | tf_op | source)
XLA Modules:
  0.0 43.2 jit_solution(1454718975667529886)
XLA Ops:
  0.6 41.8 %shard_map.140 = (bf16[8,768]{1,0:T(8,128)(2,1)S(1)}, bf16[16,48,128]{2,1,0:T(8,128)(2,1)S(1)}) custom-call(s32[8]{0:T(128)} %len_hbm.1, s32[2,8]{1,0:T(2,128)} %bitcast.11, f32[2,8]{1,0:T(2,128)} %bitcast.12, s32[8]{0:T(128)} %mrows_hbm.1, s32[8]{0:T(128)} %mdest_hbm.1, bf16[6,8,128]{2,1,0:T(8,128)(2,1)} %bitcast.9, bf16[8,768,128]{2,1,0:T(8,128)(2,1)} %bitcast.8, ...), custom_call_target="tpu_custom_call" | custom-call | flops 2088763392 | bytes 21000000 | tf_op jit(solution)/shard_map/pallas_call | solution.py:517
  42.5 0.7 %shard_map.141 = (bf16[8,768]{1,0:T(8,128)(2,1)}, bf16[16,48,128]{2,1,0:T(8,128)(2,1)}) custom-call(bf16[8,768]{1,0:T(8,128)(2,1)S(1)} %get-tuple-element.6.mixed_in, bf16[16,48,128]{2,1,0:T(8,128)(2,1)S(1)} %get-tuple-element.7.landed_in), custom_call_target="tpu_custom_call" | custom-call | tf_op jit(solution)/shard_map/pallas_call | solution.py:607

commit v4 on v3

--- a/solution.py
+++ b/solution.py
@@ -18,6 +18,8 @@
 HD = 128
 SPAN = 384
 HID = 256
+FAR = [(2, 2), (2, 1), (2, 3), (1, 2), (3, 2)]
+NEAR = [(1, 1), (1, 3), (3, 1), (3, 3), (2, 0), (0, 2), (1, 0), (3, 0), (0, 1), (0, 3)]
 PIECE = 48
 
 
@@ -66,8 +68,6 @@
     mig_mid,
     mig_out2,
     gate_buf,
-    gain_buf,
-    sum_v,
     a_send,
     a_recv,
     hid_v,
@@ -88,14 +88,18 @@
     mig2_r,
     gate_s,
     gate_r,
-    gain_s,
-    gain_r,
     a_s,
     a_r,
     sq_s,
     sq_r,
+    y_s,
+    y_r,
     ag_s,
     ag_r,
+    far_s,
+    far_r,
+    fwd_s,
+    fwd_r,
     agc_s,
     agc_r,
     r1_s,
@@ -132,7 +136,7 @@
         cp.start()
 
     def wo_copy(i):
-        b = (i // 2) * 2 + (c if i % 2 == 0 else 1 - c)
+        b = (t + 1 + i) % 8
         return pltpu.make_async_copy(
             wo_hbm.at[:, pl.ds(pl.multiple_of(b * BW, BW), BW)], wo_v.at[i], wo_sem.at[i]
         )
@@ -227,54 +231,28 @@
 
     lax.fori_loop(0, 16, seal_step, 0)
     mig_mid[g] = mig_out[g]
-    gain_buf[y] = gain_ref[...].astype(F32).reshape(1, BW)
-
-    def a_copy(i, j, d):
-        q = ((y + d) % 4) * 2 + (c if j == 0 else 1 - c)
-        return remote(a_send.at[i, j], a_recv.at[i, t], a_s, a_r.at[i], g, q)
-
-    def a_start(i):
-        for j in range(2):
-            for d in range(1 - j, 4):
-                a_copy(i, j, d).start()
-
-    def gain_copy(d):
-        q = (y + d) % 4
-        return remote(gain_buf.at[y], gain_buf.at[y], gain_s, gain_r, g, q * 2 + c)
+
+    def a_copy(i):
+        return remote(a_send.at[i], a_recv.at[t], a_s, a_r, g, (t + 1 + i) % 8)
 
     def mig_copy(i):
         k = (g + i) % 16
         return remote(mig_out.at[k], mig_mid.at[g], mig_s, mig_r, k, t)
 
     def project(i):
-        wo_copy(2 * i).wait()
-        part = jnp.dot(heads, wo_v[2 * i], preferred_element_type=F32)
-        part = part + jnp.where(y == i, res_v[...].astype(F32), 0.0)
-        sum_v[i] = part
-        a_send[i, 0] = part.astype(BF16)
-        wo_copy(2 * i + 1).wait()
-        part = jnp.dot(heads, wo_v[2 * i + 1], preferred_element_type=F32)
-        a_send[i, 1] = part.astype(BF16)
-
-    project(0)
-    project(1)
+        wo_copy(i).wait()
+        return jnp.dot(heads, wo_v[i], preferred_element_type=F32)
+
+    for i in range(6):
+        a_send[i] = project(i).astype(BF16)
     pl.semaphore_wait(barrier, 13)
-    a_start(0)
+    for i in range(6):
+        a_copy(i).start()
     for d in range(1, 4):
         greet(ready, z * 4 + (x + d) % 4, t)
-    for d in range(1, 4):
-        gain_copy(d).start()
-    a_start(1)
-    project(2)
-    a_start(2)
-    project(3)
-    a_start(3)
-
-    pl.semaphore_wait(ready, 3)
-
-    @pl.loop(1, 16)
-    def _(i):
-        mig_copy(i).start()
+    a_send[6] = project(6).astype(BF16)
+    a_copy(6).start()
+    hidden = res_v[...].astype(F32) + project(7)
 
     sub = lax.broadcasted_iota(jnp.int32, (ROWS, 128), 0)
     lane = lax.broadcasted_iota(jnp.int32, (ROWS, 128), 1)
@@ -285,31 +263,96 @@
                 jnp.logical_and(sub == r, lane == eids[k, r]), gates[k, r], gate_rows
             )
 
-    def ag_copy(i, d):
+    def plane(off):
+        return ((z + off[0]) % 4) * 4 + (x + off[1]) % 4
+
+    def y_copy(d):
         return remote(
-            xb.at[c, i, g], xb.at[c, i, g], ag_s, ag_r.at[i], (g + d) % 16, t
-        )
-
-    taken(gain_buf.at[pl.ds(0, 3)], gain_r)
-    squares = jnp.zeros((ROWS, 1), F32)
-    for i in range(4):
-        taken(a_recv.at[i, pl.ds(0, 7)], a_r.at[i])
-        hidden = sum_v[i]
-        for d in range(1, 8):
-            hidden = hidden + a_recv[i, (t + d) % 8].astype(F32)
-        hid_v[i] = hidden
-        squares = squares + jnp.sum(hidden * hidden, axis=1, keepdims=True)
-        xb[c, i, g] = (hidden * gain_buf[i]).astype(BF16)
-
-        @pl.loop(1, 16)
-        def _(d):
-            ag_copy(i, d).start()
-
-    sq_buf[0] = jnp.broadcast_to(squares, (ROWS, 128))
-    sq_copy = remote(sq_buf.at[0], sq_buf.at[1], sq_s, sq_r, g, partner)
-    sq_copy.start()
-    taken(sq_buf.at[1], sq_r)
-    scale = lax.rsqrt((sq_buf[0] + sq_buf[1]) / D + 1e-05)
+            xb.at[c, y, g], xb.at[c, y, g], y_s, y_r.at[y], g, ((y + d) % 4) * 2 + c
+        )
+
+    def ag_copy(yb, off):
+        return remote(
+            xb.at[c, yb, g], xb.at[c, yb, g], ag_s, ag_r.at[yb], plane(off), t
+        )
+
+    def far_copy(off):
+        return remote(xb.at[c, y, g], xb.at[c, y, g], far_s, far_r, plane(off), t)
+
+    def fwd_copy(off, d):
+        k = plane(off)
+        return remote(
+            xb.at[c, y, k],
+            xb.at[c, y, k],
+            fwd_s,
+            fwd_r.at[y],
+            g,
+            ((y + d) % 4) * 2 + c,
+        )
+
+    def sq_copy(d):
+        return remote(sq_buf.at[t], sq_buf.at[t], sq_s, sq_r, g, (t + d) % 8)
+
+    pl.semaphore_wait(ready, 3)
+
+    @pl.loop(1, 16)
+    def _(i):
+        mig_copy(i).start()
+
+    wi_cp.wait()
+    ri = lax.broadcasted_iota(jnp.int32, (256, 256), 0)
+    ci = lax.broadcasted_iota(jnp.int32, (256, 256), 1)
+    spot = jnp.where(ri < 128, 2 * ri, 2 * ri - 255)
+    apart = jnp.where(spot == ci, 1.0, 0.0).astype(BF16)
+
+    def apart_step(k, _):
+        pairs = wi_v[pl.ds(pl.multiple_of(k * 256, 256), 256), :]
+        rows = jnp.dot(apart, pairs, preferred_element_type=F32).astype(BF16)
+        at = pl.ds(pl.multiple_of(k * 128, 128), 128)
+        wi2_v[at, 0:HID] = rows[0:128]
+        wi2_v[at, HID : 2 * HID] = rows[128:256]
+        return 0
+
+    lax.fori_loop(0, D // 256, apart_step, 0, unroll=4)
+
+    taken(a_recv.at[pl.ds(0, 7)], a_r)
+    for d in range(1, 8):
+        hidden = hidden + a_recv[(t + d) % 8].astype(F32)
+    hid_v[...] = hidden
+    scaled = hidden * gain_ref[...].astype(F32).reshape(1, BW)
+    xb[c, y, g] = scaled.astype(BF16)
+    for d in range(1, 4):
+        y_copy(d).start()
+    for off in FAR:
+        far_copy(off).start()
+    for off in NEAR:
+        ag_copy(y, off).start()
+    squares = jnp.sum(hidden * hidden, axis=1, keepdims=True)
+    sq_buf[t] = jnp.broadcast_to(squares, (ROWS, 128))
+    for d in range(1, 8):
+        sq_copy(d).start()
+
+    lax.fori_loop(D // 256, D // 128, apart_step, 0, unroll=4)
+
+    def pass_on(j, _):
+        yb = (y + 4 - j) % 4
+        taken(xb.at[c, yb, g], y_r.at[yb])
+        for off in NEAR:
+            ag_copy(yb, off).start()
+        return 0
+
+    lax.fori_loop(1, 4, pass_on, 0)
+
+    taken(xb.at[c, y, pl.ds(0, 5)], far_r)
+    for off in FAR:
+        for d in range(1, 4):
+            fwd_copy(off, d).start()
+
+    taken(sq_buf.at[pl.ds(0, 7)], sq_r)
+    total = sq_buf[0]
+    for k in range(1, 8):
+        total = total + sq_buf[k]
+    scale = lax.rsqrt(total / D + 1e-05)
     gate_buf[g] = jnp.where(lane == EXPERTS, scale, gate_rows)
 
     def gate_copy(i):
@@ -342,26 +385,14 @@
     keep = pltpu.make_async_copy(mig_out2.at[g], landed.at[g], loc_sem)
     keep.start()
 
-    sent(a_recv.at[:, pl.ds(0, 7)], a_s)
-    sent(gain_buf.at[pl.ds(0, 3)], gain_s)
+    @pl.loop(1, 16)
+    def _(i):
+        mig2_copy((g + i) % 16).start()
+
+
+    sent(a_send, a_s)
     sent(mig_out.at[pl.ds(0, 15)], mig_s)
-    sent(sq_buf.at[0], sq_s)
-
-    wi_cp.wait()
-    ri = lax.broadcasted_iota(jnp.int32, (256, 256), 0)
-    ci = lax.broadcasted_iota(jnp.int32, (256, 256), 1)
-    spot = jnp.where(ri < 128, 2 * ri, 2 * ri - 255)
-    apart = jnp.where(spot == ci, 1.0, 0.0).astype(BF16)
-
-    def apart_step(k, _):
-        pairs = wi_v[pl.ds(pl.multiple_of(k * 256, 256), 256), :]
-        rows = jnp.dot(apart, pairs, preferred_element_type=F32).astype(BF16)
-        at = pl.ds(pl.multiple_of(k * 128, 128), 128)
-        wi2_v[at, 0:HID] = rows[0:128]
-        wi2_v[at, HID : 2 * HID] = rows[128:256]
-        return 0
-
-    lax.fori_loop(0, D // 128, apart_step, 0, unroll=4)
+    sent(sq_buf.at[pl.ds(0, 7)], sq_s)
 
     def agc_copy(i):
         return remote(xb.at[c, i], xb.at[c, i], agc_s, agc_r.at[i], g, partner)
@@ -376,27 +407,34 @@
 
     acc_v[...] = jnp.zeros_like(acc_v)
 
-    def up_step(yb, _):
-        @pl.when(yb < 4)
-        def _():
-            taken(xb.at[c, yb, pl.ds(0, 15)], ag_r.at[yb])
-            agc_copy(yb).start()
-            up_part(c, yb)
-
-        @pl.when(yb == 4)
-        def _():
-            @pl.loop(1, 16)
-            def _(i):
-                mig2_copy((g + i) % 16).start()
-
-        @pl.when(yb > 0)
-        def _():
-            taken(xb.at[1 - c, yb - 1], agc_r.at[yb - 1])
-            up_part(1 - c, yb - 1)
-
-        return 0
-
-    lax.fori_loop(0, 5, up_step, 0)
+    taken(xb.at[c, y, pl.ds(0, 10)], ag_r.at[y])
+    agc_copy(y).start()
+    up_part(c, y)
+    taken(xb.at[1 - c, y], agc_r.at[y])
+    up_part(1 - c, y)
+
+    def arrive_step(j, _):
+        yb = (y + 4 - j) % 4
+        taken(xb.at[c, yb, pl.ds(0, 10)], ag_r.at[yb])
+        taken(xb.at[c, yb, pl.ds(0, 5)], fwd_r.at[yb])
+        agc_copy(yb).start()
+        return 0
+
+    lax.fori_loop(1, 4, arrive_step, 0)
+
+    def own_step(j, _):
+        up_part(c, (y + 4 - j) % 4)
+        return 0
+
+    lax.fori_loop(1, 4, own_step, 0)
+
+    def other_step(j, _):
+        yb = (y + 4 - j) % 4
+        taken(xb.at[1 - c, yb], agc_r.at[yb])
+        up_part(1 - c, yb)
+        return 0
+
+    lax.fori_loop(1, 4, other_step, 0)
 
     taken(gate_buf.at[pl.ds(0, 15)], gate_r)
     gate_all = jnp.concatenate([gate_buf[k] for k in range(16)], axis=0)
@@ -421,8 +459,11 @@
     def r1_copy(yb):
         return remote(r1_send.at[yb], r1_recv.at[yb], r1_s, r1_r.at[yb], g, partner)
 
+    def block_at(j):
+        return (y + jnp.where(j == 0, 2, jnp.where(j == 1, 1, jnp.where(j == 2, 3, 0)))) % 4
+
     def r1_step(j, _):
-        yb = (y + 1 + j) % 4
+        yb = block_at(j)
         part = down(1 - c, yb)
         for k in range(16):
             r1_send[yb, k] = part[k * ROWS : (k + 1) * ROWS].astype(BF16)
@@ -437,16 +478,15 @@
         )
 
     def r2_step(j, _):
-        yb = (y + 1 + j) % 4
+        yb = block_at(j)
         part = down(c, yb)
         taken(r1_recv.at[yb], r1_r.at[yb])
         for k in range(16):
             both = part[k * ROWS : (k + 1) * ROWS] + r1_recv[yb, k].astype(F32)
             r2_send[yb, k] = both.astype(BF16)
 
-        @pl.loop(1, 16)
-        def _(i):
-            r2_copy(j, yb, (g + i) % 16).start()
+        for dz, dx in FAR + NEAR:
+            r2_copy(j, yb, ((z + dz) % 4) * 4 + (x + dx) % 4).start()
 
         @pl.when(j < 3)
         def _():
@@ -460,11 +500,14 @@
     taken(landed.at[pl.ds(0, 15)], mig2_r)
     sent(mig_out2.at[pl.ds(0, 15)], mig2_s)
     sent(gate_buf.at[pl.ds(0, 15)], gate_s)
-    sent(xb.at[0, :, pl.ds(0, 15)], ag_s)
+    sent(xb.at[0, 0, pl.ds(0, 3)], y_s)
+    sent(xb.at[0, :, pl.ds(0, 10)], ag_s)
+    sent(xb.at[0, 0, pl.ds(0, 5)], far_s)
+    sent(xb.at[0, 0, pl.ds(0, 15)], fwd_s)
     sent(xb.at[0], agc_s)
     sent(r1_send, r1_s)
 
-    result = hid_v[y] + r2_send[y, g].astype(F32)
+    result = hid_v[...] + r2_send[y, g].astype(F32)
 
     def add_from(s, first_g, count, total):
         def step(i, acc):
@@ -472,8 +515,8 @@
 
         return lax.fori_loop(0, count, step, total, unroll=True)
 
-    for j in range(3):
-        s = (y + 3 - j) % 4
+    for j in (2, 3, 1):
+        s = (y + j) % 4
         taken(r2_recv.at[s], r2_r.at[s])
         result = add_from(s, 0, 16, result)
     taken(r2_recv.at[y, pl.ds(0, 15)], r2_r.at[y])
@@ -541,12 +584,10 @@
             vmem((16, PIECE, HD), BF16),
             vmem((16, PIECE, HD), BF16),
             vmem((16, ROWS, 128), F32),
-            vmem((4, 1, BW), F32),
-            vmem((4, ROWS, BW), F32),
-            vmem((4, 2, ROWS, BW), BF16),
-            vmem((4, 8, ROWS, BW), BF16),
-            vmem((4, ROWS, BW), F32),
-            vmem((2, ROWS, 128), F32),
+            vmem((7, ROWS, BW), BF16),
+            vmem((8, ROWS, BW), BF16),
+            vmem((ROWS, BW), F32),
+            vmem((8, ROWS, 128), F32),
             vmem((2, 4, 16, ROWS, BW), BF16),
             vmem((128, HID), BF16),
             vmem((128, 2 * HID), F32),
@@ -565,6 +606,10 @@
             dma,
             dma,
             dma,
+            dma,
+            dma,
+            dma,
+            dma((4,)),
             dma,
             dma((4,)),
             dma,

time: 43.4 us -> 42.1 us (0.970); the launches traced: 43.2 us -> 41.3 us
  Pallas kernels: 42.5 us -> 40.7 us
    pallas_call x1, Pallas kernels: 41.8 us -> 40 us  [body(): pl.pallas_call(kernel, out_shape=(pltpu.VMEM((ROWS, BW), BF16), pltpu.VME...]
where the time goes in v4:
time: 42.1 us; the launch traced here: 41.3 us
  Pallas kernels  40.7 us (97%)
  between operations  0.64 us (2%)
    pallas_call x1, Pallas kernels, body(): pl.pallas_call(kernel, out_shape=(pltpu.VMEM((ROWS, BW), BF16), pltpu.VME...  40 us

profile of v4, /device:TPU:0, one launch (start us, length us, event | category | flops | bytes accessed | tf_op | source)
XLA Modules:
  0.0 41.3 jit_solution(304809016671100040)
XLA Ops:
  0.6 40.0 %shard_map.140 = (bf16[8,768]{1,0:T(8,128)(2,1)S(1)}, bf16[16,48,128]{2,1,0:T(8,128)(2,1)S(1)}) custom-call(s32[8]{0:T(128)} %len_hbm.1, s32[2,8]{1,0:T(2,128)} %bitcast.11, f32[2,8]{1,0:T(2,128)} %bitcast.12, s32[8]{0:T(128)} %mrows_hbm.1, s32[8]{0:T(128)} %mdest_hbm.1, bf16[6,8,128]{2,1,0:T(8,128)(2,1)} %bitcast.9, bf16[8,768,128]{2,1,0:T(8,128)(2,1)} %bitcast.8, ...), custom_call_target="tpu_custom_call" | custom-call | flops 2088763392 | bytes 21000000 | tf_op jit(solution)/shard_map/pallas_call | solution.py:560
  40.6 0.7 %shard_map.141 = (bf16[8,768]{1,0:T(8,128)(2,1)}, bf16[16,48,128]{2,1,0:T(8,128)(2,1)}) custom-call(bf16[8,768]{1,0:T(8,128)(2,1)S(1)} %get-tuple-element.6.mixed_in, bf16[16,48,128]{2,1,0:T(8,128)(2,1)S(1)} %get-tuple-element.7.landed_in), custom_call_target="tpu_custom_call" | custom-call | tf_op jit(solution)/shard_map/pallas_call | solution.py:652

commit v5 on v4

--- a/solution.py
+++ b/solution.py
@@ -313,7 +313,7 @@
         wi2_v[at, HID : 2 * HID] = rows[128:256]
         return 0
 
-    lax.fori_loop(0, D // 256, apart_step, 0, unroll=4)
+    lax.fori_loop(0, 12, apart_step, 0, unroll=4)
 
     taken(a_recv.at[pl.ds(0, 7)], a_r)
     for d in range(1, 8):
@@ -332,7 +332,7 @@
     for d in range(1, 8):
         sq_copy(d).start()
 
-    lax.fori_loop(D // 256, D // 128, apart_step, 0, unroll=4)
+    lax.fori_loop(12, 48, apart_step, 0, unroll=4)
 
     def pass_on(j, _):
         yb = (y + 4 - j) % 4
@@ -426,15 +426,7 @@
         up_part(c, (y + 4 - j) % 4)
         return 0
 
-    lax.fori_loop(1, 4, own_step, 0)
-
-    def other_step(j, _):
-        yb = (y + 4 - j) % 4
-        taken(xb.at[1 - c, yb], agc_r.at[yb])
-        up_part(1 - c, yb)
-        return 0
-
-    lax.fori_loop(1, 4, other_step, 0)
+    lax.fori_loop(1, 4, own_step, 0, unroll=True)
 
     taken(gate_buf.at[pl.ds(0, 15)], gate_r)
     gate_all = jnp.concatenate([gate_buf[k] for k in range(16)], axis=0)
@@ -444,6 +436,15 @@
         jnp.where(lane_all == expert, gate_all, 0.0), axis=1, keepdims=True
     )
     scale_col = gate_all[:, EXPERTS : EXPERTS + 1]
+
+    def other_step(j, _):
+        yb = (y + 4 - j) % 4
+        taken(xb.at[1 - c, yb], agc_r.at[yb])
+        up_part(1 - c, yb)
+        return 0
+
+    lax.fori_loop(1, 4, other_step, 0)
+
     gate_part = acc_v[:, 0:HID] * scale_col
     up_value = acc_v[:, HID : 2 * HID] * scale_col
     silu = gate_part / (1.0 + jnp.exp(-gate_part))
@@ -470,7 +471,7 @@
         r1_copy(yb).start()
         return 0
 
-    lax.fori_loop(0, 4, r1_step, 0)
+    lax.fori_loop(0, 4, r1_step, 0, unroll=True)
 
     def r2_copy(j, yb, k):
         return remote(

time: 42.1 us -> 41.7 us (level)
  no operation moved by 1% of the time
where the time goes in v5:
time: 41.7 us; the launch traced here: 41.3 us
  Pallas kernels  40.6 us (97%)
  between operations  0.64 us (2%)
    pallas_call x1, Pallas kernels, body(): pl.pallas_call(kernel, out_shape=(pltpu.VMEM((ROWS, BW), BF16), pltpu.VME...  39.9 us

profile of v5, /device:TPU:0, one launch (start us, length us, event | category | flops | bytes accessed | tf_op | source)
XLA Modules:
  0.0 41.3 jit_solution(15547081069334655766)
XLA Ops:
  0.6 39.9 %shard_map.140 = (bf16[8,768]{1,0:T(8,128)(2,1)S(1)}, bf16[16,48,128]{2,1,0:T(8,128)(2,1)S(1)}) custom-call(s32[8]{0:T(128)} %len_hbm.1, s32[2,8]{1,0:T(2,128)} %bitcast.11, f32[2,8]{1,0:T(2,128)} %bitcast.12, s32[8]{0:T(128)} %mrows_hbm.1, s32[8]{0:T(128)} %mdest_hbm.1, bf16[6,8,128]{2,1,0:T(8,128)(2,1)} %bitcast.9, bf16[8,768,128]{2,1,0:T(8,128)(2,1)} %bitcast.8, ...), custom_call_target="tpu_custom_call" | custom-call | flops 2088763392 | bytes 21000000 | tf_op jit(solution)/shard_map/pallas_call | solution.py:561
  40.6 0.7 %shard_map.141 = (bf16[8,768]{1,0:T(8,128)(2,1)}, bf16[16,48,128]{2,1,0:T(8,128)(2,1)}) custom-call(bf16[8,768]{1,0:T(8,128)(2,1)S(1)} %get-tuple-element.6.mixed_in, bf16[16,48,128]{2,1,0:T(8,128)(2,1)S(1)} %get-tuple-element.7.landed_in), custom_call_target="tpu_custom_call" | custom-call | tf_op jit(solution)/shard_map/pallas_call | solution.py:653

commit v6 on v5

--- a/solution.py
+++ b/solution.py
@@ -75,6 +75,7 @@
     xb,
     act_v,
     acc_v,
+    part_v,
     r1_send,
     r1_recv,
     r2_send,
@@ -480,8 +481,13 @@
 
     def r2_step(j, _):
         yb = block_at(j)
-        part = down(c, yb)
+
+        @pl.when(j < 3)
+        def _():
+            part_v[(j + 1) % 2] = down(c, block_at(j + 1))
+
         taken(r1_recv.at[yb], r1_r.at[yb])
+        part = part_v[j % 2]
         for k in range(16):
             both = part[k * ROWS : (k + 1) * ROWS] + r1_recv[yb, k].astype(F32)
             r2_send[yb, k] = both.astype(BF16)
@@ -495,6 +501,7 @@
 
         return 0
 
+    part_v[0] = down(c, block_at(0))
     lax.fori_loop(0, 4, r2_step, 0)
 
     keep.wait()
@@ -592,6 +599,7 @@
             vmem((2, 4, 16, ROWS, BW), BF16),
             vmem((128, HID), BF16),
             vmem((128, 2 * HID), F32),
+            vmem((2, 128, BW), F32),
             vmem((4, 16, ROWS, BW), BF16),
             vmem((4, 16, ROWS, BW), BF16),
             vmem((4, 16, ROWS, BW), BF16),

time: 41.7 us -> 41.6 us (level)
  no operation moved by 1% of the time
where the time goes in v6:
time: 41.6 us; the launch traced here: 41.1 us
  Pallas kernels  40.5 us (97%)
  between operations  0.64 us (2%)
    pallas_call x1, Pallas kernels, body(): pl.pallas_call(kernel, out_shape=(pltpu.VMEM((ROWS, BW), BF16), pltpu.VME...  39.8 us

profile of v6, /device:TPU:0, one launch (start us, length us, event | category | flops | bytes accessed | tf_op | source)
XLA Modules:
  0.0 41.1 jit_solution(4137796676666725725)
XLA Ops:
  0.6 39.8 %shard_map.140 = (bf16[8,768]{1,0:T(8,128)(2,1)S(1)}, bf16[16,48,128]{2,1,0:T(8,128)(2,1)S(1)}) custom-call(s32[8]{0:T(128)} %len_hbm.1, s32[2,8]{1,0:T(2,128)} %bitcast.11, f32[2,8]{1,0:T(2,128)} %bitcast.12, s32[8]{0:T(128)} %mrows_hbm.1, s32[8]{0:T(128)} %mdest_hbm.1, bf16[6,8,128]{2,1,0:T(8,128)(2,1)} %bitcast.9, bf16[8,768,128]{2,1,0:T(8,128)(2,1)} %bitcast.8, ...), custom_call_target="tpu_custom_call" | custom-call | flops 2088763392 | bytes 21000000 | tf_op jit(solution)/shard_map/pallas_call | solution.py:568
  40.4 0.7 %shard_map.141 = (bf16[8,768]{1,0:T(8,128)(2,1)}, bf16[16,48,128]{2,1,0:T(8,128)(2,1)}) custom-call(bf16[8,768]{1,0:T(8,128)(2,1)S(1)} %get-tuple-element.6.mixed_in, bf16[16,48,128]{2,1,0:T(8,128)(2,1)S(1)} %get-tuple-element.7.landed_in), custom_call_target="tpu_custom_call" | custom-call | tf_op jit(solution)/shard_map/pallas_call | solution.py:661
